TPU v7x, 1024 devices: a whole 4x4x32 slice. The times are simulated.
1024 devices in a mesh: grp: 16 (over x, y_lo, core), blk: 64 (over y_hi, z).
Axes of the slice: x: 4, y: 4 (y_hi: 2, y_lo: 2; y = y_hi * 2 + y_lo), z: 32, core: 2. Of those that a mesh axis runs over, the one named last changes fastest.
Arguments:
- picture_embeds: bfloat16 [131072, 1152], P(('grp', 'blk')), may hold values from -1 to 1
- caption_embeds: bfloat16 [131072, 1152], P(('grp', 'blk')), may hold values from -1 to 1
- holder_position: int32 [131072], P(('grp', 'blk')), may hold values from 0 to 63, as said below
- score_scaling: float32 [1], replicated, may hold values from 2 to 5
- score_offset_term: float32 [1], replicated, may hold values from -3 to 0
Outputs:
- image_grad: bfloat16 [131072, 1152], P(('grp', 'blk'))
- text_grad: bfloat16 [131072, 1152], P(('grp', 'blk'))
Inputs may be any that keep to these rules, and one draw needn't show every extreme that they name: `holder_position`: of the 128 rows of one device at most 4 name any one position; in each group some position is named by exactly 4 rows of every device of the group.
All inputs are finite; a program needn't handle non-finite values.
Results may differ from a plain program's by a relative error of at most 0.005.
Values may be sent and summed in bfloat16 or wider, within the bound.
No kernel may reach another device: no remote copies, remote signals or barrier semaphores. Data moves between devices by JAX's collectives and lax.ppermute only.
A program may use at most 32 MiB of HBM per device.

v0:
```python
import jax
import jax.numpy as jnp
from jax import lax
from jax.sharding import PartitionSpec as P

STEPS = 2


def shifted(x, axis, by):
    devices = lax.axis_size(axis)
    return lax.ppermute(x, axis, [(i, (i + by) % devices) for i in range(devices)])


def weight_matrix(
    picture_batch, caption_batch, sharpness_multiplier, start_displacement, matching_label
):
    pair_scores = (
        sharpness_multiplier
        * lax.dot_general(
            picture_batch,
            caption_batch,
            (((1,), (1,)), ((), ())),
            preferred_element_type=jnp.float32,
        )
        + start_displacement
    )
    return (sharpness_multiplier * (jax.nn.sigmoid(pair_scores) - matching_label)).astype(
        jnp.bfloat16
    )


def image_part(weight_entry, caption_batch):
    return jnp.dot(weight_entry, caption_batch, preferred_element_type=jnp.float32)


def text_part(weight_entry, picture_batch):
    return lax.dot_general(
        weight_entry, picture_batch, (((0,), (0,)), ((), ())), preferred_element_type=jnp.float32
    )


def body(picture_embeds, caption_embeds, holder_position, score_scaling, score_offset_term):
    rows_here = picture_embeds.shape[0]
    width = picture_embeds.shape[1]
    blk_count = lax.axis_size("blk")
    capacity = 2 * rows_here // blk_count
    slots = blk_count * capacity
    sharpness_multiplier = score_scaling[0]
    start_displacement = score_offset_term[0]
    dest_hit = (holder_position[:, None] == jnp.arange(blk_count, dtype=jnp.int32)[None, :]).astype(
        jnp.int32
    )
    rank_in = jnp.sum(jnp.cumsum(dest_hit, axis=0) * dest_hit, axis=1) - 1
    slot_lookup = holder_position * capacity + rank_in
    placer = (jnp.arange(slots, dtype=jnp.int32)[:, None] == slot_lookup[None, :]).astype(
        jnp.bfloat16
    )
    image_send = jnp.dot(placer, picture_embeds, preferred_element_type=jnp.float32).astype(
        jnp.bfloat16
    )
    text_send = jnp.dot(placer, caption_embeds, preferred_element_type=jnp.float32).astype(
        jnp.bfloat16
    )
    image_recv, text_received = (
        lax.all_to_all(
            image_send.reshape(blk_count, capacity, width),
            "blk",
            split_axis=0,
            concat_axis=0,
            tiled=True,
        ),
        lax.all_to_all(
            text_send.reshape(blk_count, capacity, width),
            "blk",
            split_axis=0,
            concat_axis=0,
            tiled=True,
        ),
    )
    picture_batch = image_recv.reshape(slots, width)
    mine_caption_batch = text_received.reshape(slots, width)
    identity_square = jnp.eye(slots, dtype=jnp.float32)
    weight_entry = weight_matrix(
        picture_batch, mine_caption_batch, sharpness_multiplier, start_displacement, identity_square
    )
    image_total = image_part(weight_entry, mine_caption_batch)
    own_part = text_part(weight_entry, picture_batch)
    guest_caption_batch = mine_caption_batch
    text_acc = own_part
    for step in range(STEPS):
        guest_caption_batch, text_acc = (
            shifted(guest_caption_batch.astype(jnp.float32), ("grp", "blk"), 1).astype(
                guest_caption_batch.dtype
            ),
            shifted(text_acc, ("grp", "blk"), 1),
        )
        weight_entry = weight_matrix(
            picture_batch,
            guest_caption_batch,
            sharpness_multiplier,
            start_displacement,
            jnp.float32(0.0),
        )
        image_total = image_total + image_part(weight_entry, guest_caption_batch)
        text_acc = text_acc + text_part(weight_entry, picture_batch)
    text_done = shifted(text_acc.astype(jnp.bfloat16), ("grp", "blk"), -STEPS)
    image_done = image_total.astype(jnp.bfloat16)
    image_back, text_back = (
        lax.all_to_all(
            image_done.reshape(blk_count, capacity, width),
            "blk",
            split_axis=0,
            concat_axis=0,
            tiled=True,
        ),
        lax.all_to_all(
            text_done.reshape(blk_count, capacity, width),
            "blk",
            split_axis=0,
            concat_axis=0,
            tiled=True,
        ),
    )
    image_grad = text_part(placer, image_back.reshape(slots, width)).astype(jnp.bfloat16)
    text_grad = text_part(placer, text_back.reshape(slots, width)).astype(jnp.bfloat16)
    return (image_grad, text_grad)


def solution(mesh):
    placed = (P(("grp", "blk"), None), P(("grp", "blk"), None), P(("grp", "blk")), P(), P())
    return jax.shard_map(
        body,
        mesh=mesh,
        in_specs=placed,
        out_specs=(P(("grp", "blk"), None), P(("grp", "blk"), None)),
        check_vma=False,
    )
```

profile of v0, /device:TPU:98, one launch (start us, length us, event | category | flops | bytes accessed | tf_op | source)
XLA Modules:
  0.0 450.4 jit_solution(14615902359415850249)
XLA Ops:
  0.6 0.0 copy-start
  0.6 0.8 fusion.29
  1.4 0.2 reduce_window_sum.11
  1.6 0.8 select_reduce_fusion
  2.4 0.7 add_add_fusion
  3.1 0.0 copy-done
  3.1 0.3 convolution_convert_fusion
  3.4 0.0 copy-start.1
  3.4 1.0 reshape.32
  4.4 30.7 %all-to-all-start.1 = ((bf16[64,4,1152]{2,1,0:T(4,128)(2,1)}), bf16[64,4,1152]{2,1,0:T(4,128)(2,1)S(1)}, u32[]{:S(2)}, u32[]{:S(2)}) async-start(bf16[64,4,1152]{2,1,0:T(4,128)(2,1)} %reshape.32), calls=%async_computation.1 | async-start | bytes 1179648 | tf_op jit(solution)/shard_map/all_to_all | solution.py:72
  35.1 0.0 copy-done.1
  35.1 0.3 convolution_convert_fusion.1
  35.4 1.0 reshape.30
  36.4 67.6 %all-to-all-done.1 = bf16[64,4,1152]{2,1,0:T(4,128)(2,1)S(1)} async-done(((bf16[64,4,1152]{2,1,0:T(4,128)(2,1)}), bf16[64,4,1152]{2,1,0:T(4,128)(2,1)S(1)}, u32[]{:S(2)}, u32[]{:S(2)}) %all-to-all-start.1) | async-done | bytes 589856 | tf_op jit(solution)/shard_map/all_to_all | solution.py:72
  104.0 7.1 %all-to-all-start = ((bf16[64,4,1152]{2,1,0:T(4,128)(2,1)}), bf16[64,4,1152]{2,1,0:T(4,128)(2,1)S(1)}, u32[]{:S(2)}, u32[]{:S(2)}) async-start(bf16[64,4,1152]{2,1,0:T(4,128)(2,1)} %reshape.30), calls=%async_computation | async-start | bytes 1179648 | tf_op jit(solution)/shard_map/all_to_all | solution.py:65
  111.1 0.1 reshape.33
  111.2 4.6 %collective-permute-start = (bf16[256,1152]{1,0:T(8,128)(2,1)S(1)}, bf16[256,1152]{1,0:T(8,128)(2,1)S(1)}, u32[]{:S(2)}, u32[]{:S(2)}) collective-permute-start(bf16[256,1152]{1,0:T(8,128)(2,1)S(1)} %reshape.33), channel_id=1, source_target_pairs={{0,1},{1,2},{2,3},{3,4},{4,5},{5,6},{6,7},{7,8},{8,9},{9,10},{10,1... | collective-permute-start | bytes 1769480 | tf_op jit(solution)/shard_map/ppermute | solution.py:11
  117.1 62.6 %all-to-all-done = bf16[64,4,1152]{2,1,0:T(4,128)(2,1)S(1)} async-done(((bf16[64,4,1152]{2,1,0:T(4,128)(2,1)}), bf16[64,4,1152]{2,1,0:T(4,128)(2,1)S(1)}, u32[]{:S(2)}, u32[]{:S(2)}) %all-to-all-start) | async-done | bytes 589856 | tf_op jit(solution)/shard_map/all_to_all | solution.py:65
  179.7 0.1 reshape.31
  179.8 0.4 fusion.20
  180.2 0.0 collective-permute-done
  180.2 1.9 collective-permute-start.1
  182.2 0.3 fusion.32
  182.5 0.4 fusion.21
  182.9 0.3 convolution_add_fusion.2
  183.3 12.8 %collective-permute-done.1 = bf16[256,1152]{1,0:T(8,128)(2,1)S(1)} collective-permute-done((bf16[256,1152]{1,0:T(8,128)(2,1)S(1)}, bf16[256,1152]{1,0:T(8,128)(2,1)S(1)}, u32[]{:S(2)}, u32[]{:S(2)}) %collective-permute-start.1) | collective-permute-done | bytes 589856 | tf_op jit(solution)/shard_map/ppermute | solution.py:11
  196.1 0.4 fusion.22
  196.5 0.3 fusion
  196.8 1.0 reshape.34
  197.8 21.5 %all-to-all-start.2 = ((bf16[64,4,1152]{2,1,0:T(4,128)(2,1)}), bf16[64,4,1152]{2,1,0:T(4,128)(2,1)S(1)}, u32[]{:S(2)}, u32[]{:S(2)}) async-start(bf16[64,4,1152]{2,1,0:T(4,128)(2,1)} %reshape.34), calls=%async_computation.2 | async-start | bytes 1179648 | tf_op jit(solution)/shard_map/all_to_all | solution.py:109
  219.3 0.4 fusion.33
  219.7 4.6 %collective-permute-start.2 = (f32[256,1152]{1,0:T(8,128)S(1)}, f32[256,1152]{1,0:T(8,128)S(1)}, u32[]{:S(2)}, u32[]{:S(2)}) collective-permute-start(f32[256,1152]{1,0:T(8,128)S(1)} %fusion.33), channel_id=1, source_target_pairs={{0,1},{1,2},{2,3},{3,4},{4,5},{5,6},{6,7},{7,8},{8,9},{9,10},{10,1... | collective-permute-start | bytes 3538952 | tf_op jit(solution)/shard_map/ppermute | solution.py:11
  224.3 70.6 %collective-permute-done.2 = f32[256,1152]{1,0:T(8,128)S(1)} collective-permute-done((f32[256,1152]{1,0:T(8,128)S(1)}, f32[256,1152]{1,0:T(8,128)S(1)}, u32[]{:S(2)}, u32[]{:S(2)}) %collective-permute-start.2) | collective-permute-done | bytes 1179680 | tf_op jit(solution)/shard_map/ppermute | solution.py:11
  294.8 0.4 convolution_add_fusion
  295.2 4.6 %collective-permute-start.3 = (f32[256,1152]{1,0:T(8,128)S(1)}, f32[256,1152]{1,0:T(8,128)S(1)}, u32[]{:S(2)}, u32[]{:S(2)}) collective-permute-start(f32[256,1152]{1,0:T(8,128)S(1)} %convolution_add_fusion), channel_id=1, source_target_pairs={{0,1},{1,2},{2,3},{3,4},{4,5},{5,6},{6,7},{7,8},{8,9},{9,10},{10,1... | collective-permute-start | bytes 3538952 | tf_op jit(solution)/shard_map/ppermute | solution.py:11
  299.8 0.4 fusion.34
  300.2 25.0 %collective-permute-done.3 = f32[256,1152]{1,0:T(8,128)S(1)} collective-permute-done((f32[256,1152]{1,0:T(8,128)S(1)}, f32[256,1152]{1,0:T(8,128)S(1)}, u32[]{:S(2)}, u32[]{:S(2)}) %collective-permute-start.3) | collective-permute-done | bytes 1179680 | tf_op jit(solution)/shard_map/ppermute | solution.py:11
  325.2 0.1 add_convert_fusion
  325.3 5.1 %collective-permute-start.4 = (bf16[256,1152]{1,0:T(8,128)(2,1)S(1)}, bf16[256,1152]{1,0:T(8,128)(2,1)S(1)}, u32[]{:S(2)}, u32[]{:S(2)}) collective-permute-start(bf16[256,1152]{1,0:T(8,128)(2,1)S(1)} %add_convert_fusion), channel_id=1, source_target_pairs={{0,1022},{1,1023},{2,0},{3,1},{4,2},{5,3},{6,4},{7,5},{8,6},{9,7},... | collective-permute-start | bytes 1769480 | tf_op jit(solution)/shard_map/ppermute | solution.py:11
  330.3 25.3 %collective-permute-done.4 = bf16[256,1152]{1,0:T(8,128)(2,1)S(1)} collective-permute-done((bf16[256,1152]{1,0:T(8,128)(2,1)S(1)}, bf16[256,1152]{1,0:T(8,128)(2,1)S(1)}, u32[]{:S(2)}, u32[]{:S(2)}) %collective-permute-start.4) | collective-permute-done | bytes 589856 | tf_op jit(solution)/shard_map/ppermute | solution.py:11
  355.6 1.0 reshape.36
  356.6 0.0 all-to-all-done.2
  356.6 24.0 %all-to-all-start.3 = ((bf16[64,4,1152]{2,1,0:T(4,128)(2,1)}), bf16[64,4,1152]{2,1,0:T(4,128)(2,1)S(1)}, u32[]{:S(2)}, u32[]{:S(2)}) async-start(bf16[64,4,1152]{2,1,0:T(4,128)(2,1)} %reshape.36), calls=%async_computation.3 | async-start | bytes 1179648 | tf_op jit(solution)/shard_map/all_to_all | solution.py:116
  380.6 0.1 reshape.35
  380.7 1.0 convolution_convert_fusion.3
  381.8 67.5 %all-to-all-done.3 = bf16[64,4,1152]{2,1,0:T(4,128)(2,1)S(1)} async-done(((bf16[64,4,1152]{2,1,0:T(4,128)(2,1)}), bf16[64,4,1152]{2,1,0:T(4,128)(2,1)S(1)}, u32[]{:S(2)}, u32[]{:S(2)}) %all-to-all-start.3) | async-done | bytes 589856 | tf_op jit(solution)/shard_map/all_to_all | solution.py:116
  449.3 0.1 reshape.37
  449.4 1.0 convolution_convert_fusion.2
Async XLA Ops:
  0.6 2.5 copy-start
  3.4 31.7 %copy-start.1 = (bf16[128,1152]{1,0:T(8,128)(2,1)S(1)}, bf16[128,1152]{1,0:T(8,128)(2,1)}, u32[]{:S(2)}) copy-start(bf16[128,1152]{1,0:T(8,128)(2,1)} %param.5) | copy-start | bytes 884740
  4.4 99.6 %all-to-all-start.1 = ((bf16[64,4,1152]{2,1,0:T(4,128)(2,1)}), bf16[64,4,1152]{2,1,0:T(4,128)(2,1)S(1)}, u32[]{:S(2)}, u32[]{:S(2)}) async-start(bf16[64,4,1152]{2,1,0:T(4,128)(2,1)} %reshape.32), calls=%async_computation.1 | async-start | bytes 1179648 | tf_op jit(solution)/shard_map/all_to_all | solution.py:72
  104.0 75.7 %all-to-all-start = ((bf16[64,4,1152]{2,1,0:T(4,128)(2,1)}), bf16[64,4,1152]{2,1,0:T(4,128)(2,1)S(1)}, u32[]{:S(2)}, u32[]{:S(2)}) async-start(bf16[64,4,1152]{2,1,0:T(4,128)(2,1)} %reshape.30), calls=%async_computation | async-start | bytes 1179648 | tf_op jit(solution)/shard_map/all_to_all | solution.py:65
  111.2 69.0 %collective-permute-start = (bf16[256,1152]{1,0:T(8,128)(2,1)S(1)}, bf16[256,1152]{1,0:T(8,128)(2,1)S(1)}, u32[]{:S(2)}, u32[]{:S(2)}) collective-permute-start(bf16[256,1152]{1,0:T(8,128)(2,1)S(1)} %reshape.33), channel_id=1, source_target_pairs={{0,1},{1,2},{2,3},{3,4},{4,5},{5,6},{6,7},{7,8},{8,9},{9,10},{10,1... | collective-permute-start | bytes 1769480 | tf_op jit(solution)/shard_map/ppermute | solution.py:11
  180.2 15.8 %collective-permute-start.1 = (bf16[256,1152]{1,0:T(8,128)(2,1)S(1)}, bf16[256,1152]{1,0:T(8,128)(2,1)S(1)}, u32[]{:S(2)}, u32[]{:S(2)}) collective-permute-start(bf16[256,1152]{1,0:T(8,128)(2,1)S(1)} %collective-permute-done), channel_id=1, source_target_pairs={{0,1},{1,2},{2,3},{3,4},{4,5},{5,6},{6,7},{7,8},{8,9},{9,10},{10,1... | collective-permute-start | bytes 1769480 | tf_op jit(solution)/shard_map/ppermute | solution.py:11
  197.8 158.8 %all-to-all-start.2 = ((bf16[64,4,1152]{2,1,0:T(4,128)(2,1)}), bf16[64,4,1152]{2,1,0:T(4,128)(2,1)S(1)}, u32[]{:S(2)}, u32[]{:S(2)}) async-start(bf16[64,4,1152]{2,1,0:T(4,128)(2,1)} %reshape.34), calls=%async_computation.2 | async-start | bytes 1179648 | tf_op jit(solution)/shard_map/all_to_all | solution.py:109
  219.7 75.2 %collective-permute-start.2 = (f32[256,1152]{1,0:T(8,128)S(1)}, f32[256,1152]{1,0:T(8,128)S(1)}, u32[]{:S(2)}, u32[]{:S(2)}) collective-permute-start(f32[256,1152]{1,0:T(8,128)S(1)} %fusion.33), channel_id=1, source_target_pairs={{0,1},{1,2},{2,3},{3,4},{4,5},{5,6},{6,7},{7,8},{8,9},{9,10},{10,1... | collective-permute-start | bytes 3538952 | tf_op jit(solution)/shard_map/ppermute | solution.py:11
  295.2 29.9 %collective-permute-start.3 = (f32[256,1152]{1,0:T(8,128)S(1)}, f32[256,1152]{1,0:T(8,128)S(1)}, u32[]{:S(2)}, u32[]{:S(2)}) collective-permute-start(f32[256,1152]{1,0:T(8,128)S(1)} %convolution_add_fusion), channel_id=1, source_target_pairs={{0,1},{1,2},{2,3},{3,4},{4,5},{5,6},{6,7},{7,8},{8,9},{9,10},{10,1... | collective-permute-start | bytes 3538952 | tf_op jit(solution)/shard_map/ppermute | solution.py:11
  325.3 30.4 %collective-permute-start.4 = (bf16[256,1152]{1,0:T(8,128)(2,1)S(1)}, bf16[256,1152]{1,0:T(8,128)(2,1)S(1)}, u32[]{:S(2)}, u32[]{:S(2)}) collective-permute-start(bf16[256,1152]{1,0:T(8,128)(2,1)S(1)} %add_convert_fusion), channel_id=1, source_target_pairs={{0,1022},{1,1023},{2,0},{3,1},{4,2},{5,3},{6,4},{7,5},{8,6},{9,7},... | collective-permute-start | bytes 1769480 | tf_op jit(solution)/shard_map/ppermute | solution.py:11
  356.6 92.7 %all-to-all-start.3 = ((bf16[64,4,1152]{2,1,0:T(4,128)(2,1)}), bf16[64,4,1152]{2,1,0:T(4,128)(2,1)S(1)}, u32[]{:S(2)}, u32[]{:S(2)}) async-start(bf16[64,4,1152]{2,1,0:T(4,128)(2,1)} %reshape.36), calls=%async_computation.3 | async-start | bytes 1179648 | tf_op jit(solution)/shard_map/all_to_all | solution.py:116
where the time goes:
time: 451 us; the launch traced here: 450 us
  waiting for transfers between devices  331 us (73%)
  starting transfers between devices  104 us (23%)
  matrix products  5.96 us (1%)
    ppermute x5, waiting for transfers between devices, shifted(): lax.ppermute(x, axis, [(i, (i + by) % devices) for i in range(devices)])  134 us
    all_to_all x1, waiting for transfers between devices, body(): lax.all_to_all(text_send.reshape(blk_count, capacity, width), 'blk', spli...  67.6 us
    all_to_all x1, waiting for transfers between devices, body(): lax.all_to_all(text_done.reshape(blk_count, capacity, width), 'blk', spli...  67.5 us
    all_to_all x1, waiting for transfers between devices, body(): lax.all_to_all(image_send.reshape(blk_count, capacity, width), 'blk', spl...  62.6 us
    all_to_all x1, starting transfers between devices, body(): lax.all_to_all(text_send.reshape(blk_count, capacity, width), 'blk', spli...  30.7 us
    all_to_all x1, starting transfers between devices, body(): lax.all_to_all(text_done.reshape(blk_count, capacity, width), 'blk', spli...  24 us
    all_to_all x1, starting transfers between devices, body(): lax.all_to_all(image_done.reshape(blk_count, capacity, width), 'blk', spl...  21.5 us
    ppermute x5, starting transfers between devices, shifted(): lax.ppermute(x, axis, [(i, (i + by) % devices) for i in range(devices)])  20.7 us
  transfers between devices with their start and end apart: 9, of which 7 were waited for; matrix products, arithmetic and copies ran while one was open for 1% of the time, Pallas kernels for 0%

commit v1 on v0

v1 whole, which is shorter than its diff:
```python
import jax
import jax.numpy as jnp
from jax import lax
from jax.sharding import PartitionSpec as P

STEPS = 2
RING = ("grp", "blk")


def shifted(x, by):
    devices = lax.axis_size(RING)
    return lax.ppermute(x, RING, [(i, (i + by) % devices) for i in range(devices)])


def weight_matrix(picture_batch, caption_batch, scale, offset, matching_label):
    scores = lax.dot_general(
        picture_batch,
        caption_batch,
        (((1,), (1,)), ((), ())),
        preferred_element_type=jnp.float32,
    )
    pair_scores = scale * scores + offset
    return (scale * (jax.nn.sigmoid(pair_scores) - matching_label)).astype(jnp.bfloat16)


def times_rows(weights, rows):
    return jnp.dot(weights, rows, preferred_element_type=jnp.float32)


def rows_of_transpose(weights, rows):
    return lax.dot_general(
        weights, rows, (((0,), (0,)), ((), ())), preferred_element_type=jnp.float32
    )


def swap_blocks(x, blk_count):
    slots, width = x.shape
    out = lax.all_to_all(
        x.reshape(blk_count, slots // blk_count, width),
        "blk",
        split_axis=0,
        concat_axis=0,
        tiled=True,
    )
    return out.reshape(slots, width)


def body(picture_embeds, caption_embeds, holder_position, score_scaling, score_offset_term):
    rows_here, width = picture_embeds.shape
    blk_count = lax.axis_size("blk")
    capacity = 2 * rows_here // blk_count
    slots = blk_count * capacity
    scale = score_scaling[0]
    offset = score_offset_term[0]
    same = holder_position[:, None] == holder_position[None, :]
    order = jnp.arange(rows_here, dtype=jnp.int32)
    rank_in = jnp.sum((same & (order[None, :] < order[:, None])).astype(jnp.int32), axis=1)
    slot_lookup = holder_position * capacity + rank_in
    placer = (jnp.arange(slots, dtype=jnp.int32)[:, None] == slot_lookup[None, :]).astype(
        jnp.bfloat16
    )
    both = jnp.concatenate([picture_embeds, caption_embeds], axis=1)
    sent = times_rows(placer, both).astype(jnp.bfloat16)
    received = swap_blocks(sent, blk_count)
    pictures = received[:, :width]
    captions = received[:, width:]

    earlier_captions = [captions]
    later_pictures = [pictures]
    for _ in range(STEPS):
        earlier_captions.append(shifted(earlier_captions[-1], 1))
        later_pictures.append(shifted(later_pictures[-1], -1))

    identity_square = jnp.eye(slots, dtype=jnp.float32)
    own_weights = weight_matrix(pictures, captions, scale, offset, identity_square)
    image_total = times_rows(own_weights, captions)
    text_total = rows_of_transpose(own_weights, pictures)
    zero = jnp.float32(0.0)
    for step in range(1, STEPS + 1):
        weights = weight_matrix(pictures, earlier_captions[step], scale, offset, zero)
        image_total = image_total + times_rows(weights, earlier_captions[step])
        weights = weight_matrix(later_pictures[step], captions, scale, offset, zero)
        text_total = text_total + rows_of_transpose(weights, later_pictures[step])

    done = jnp.concatenate([image_total, text_total], axis=1).astype(jnp.bfloat16)
    back = swap_blocks(done, blk_count)
    grads = rows_of_transpose(placer, back).astype(jnp.bfloat16)
    return (grads[:, :width], grads[:, width:])


def solution(mesh):
    placed = (P(RING, None), P(RING, None), P(RING), P(), P())
    return jax.shard_map(
        body,
        mesh=mesh,
        in_specs=placed,
        out_specs=(P(RING, None), P(RING, None)),
        check_vma=False,
    )
```

time: 451 us -> 326 us (0.72)
  the two profiles are of different devices: /device:TPU:98 before, /device:TPU:102 now
where the time goes in v1:
time: 326 us
  waiting for transfers between devices  134 us (41%)
  blocking collectives  126 us (39%)
  starting transfers between devices  42.4 us (13%)
  matrix products  14.2 us (4%)
  local copies, waits for them, and re-layouts  4.38 us (1%)
    all_to_all x1, blocking collectives, swap_blocks(): lax.all_to_all(x.reshape(blk_count, slots // blk_count, width), 'blk', sp...  126 us
    all_to_all x1, waiting for transfers between devices, swap_blocks(): lax.all_to_all(x.reshape(blk_count, slots // blk_count, width), 'blk', sp...  117 us
    all_to_all x1, starting transfers between devices, swap_blocks(): lax.all_to_all(x.reshape(blk_count, slots // blk_count, width), 'blk', sp...  30.7 us
    ppermute x4, waiting for transfers between devices, shifted(): lax.ppermute(x, RING, [(i, (i + by) % devices) for i in range(devices)])  17 us
    ppermute x4, starting transfers between devices, shifted(): lax.ppermute(x, RING, [(i, (i + by) % devices) for i in range(devices)])  11.7 us
    dot_general x4, matrix products, times_rows(): return jnp.dot(weights, rows, preferred_element_type=jnp.float32)  7.6 us
  transfers between devices with their start and end apart: 5, of which 4 were waited for; matrix products, arithmetic and copies ran while one was open for 3% of the time, Pallas kernels for 0%

profile of v1, /device:TPU:102, one launch (start us, length us, event | category | flops | bytes accessed | tf_op | source)
XLA Modules:
  0.0 325.6 jit_solution(16702616275220435591)
XLA Ops:
  0.6 0.9 convert_reduce_fusion
  1.5 0.7 multiply_add_fusion
  2.2 1.5 convolution_convert_fusion
  3.7 1.2 reshape.21
  4.9 30.7 %all-to-all-start = ((bf16[64,4,2304]{2,1,0:T(4,128)(2,1)}), bf16[64,4,2304]{2,1,0:T(4,128)(2,1)S(1)}, u32[]{:S(2)}, u32[]{:S(2)}) async-start(bf16[64,4,2304]{2,1,0:T(4,128)(2,1)} %reshape.21), calls=%async_computation | async-start | bytes 2359296 | tf_op jit(solution)/shard_map/all_to_all | solution.py:38
  36.9 117.4 %all-to-all-done = bf16[64,4,2304]{2,1,0:T(4,128)(2,1)S(1)} async-done(((bf16[64,4,2304]{2,1,0:T(4,128)(2,1)}), bf16[64,4,2304]{2,1,0:T(4,128)(2,1)S(1)}, u32[]{:S(2)}, u32[]{:S(2)}) %all-to-all-start) | async-done | bytes 1179680 | tf_op jit(solution)/shard_map/all_to_all | solution.py:38
  154.3 0.3 reshape.22
  154.6 0.1 fusion.75
  154.7 1.9 collective-permute-start
  156.6 3.9 %collective-permute-start.2 = (bf16[256,1152]{1,0:T(8,128)(2,1)S(1)}, bf16[256,1152]{1,0:T(8,128)(2,1)}, u32[]{:S(2)}, u32[]{:S(2)}) collective-permute-start(bf16[256,1152]{1,0:T(8,128)(2,1)S(1)} %get-tuple-element.3), channel_id=1, source_target_pairs={{0,1023},{1,0},{2,1},{3,2},{4,3},{5,4},{6,5},{7,6},{8,7},{9,8},{10... | collective-permute-start | bytes 1769480 | tf_op jit(solution)/shard_map/ppermute | solution.py:12
  160.5 0.4 fusion.33
  160.9 0.3 fusion.65
  161.3 0.4 fusion.68
  161.7 10.1 %collective-permute-done = bf16[256,1152]{1,0:T(8,128)(2,1)} collective-permute-done((bf16[256,1152]{1,0:T(8,128)(2,1)S(1)}, bf16[256,1152]{1,0:T(8,128)(2,1)}, u32[]{:S(2)}, u32[]{:S(2)}) %collective-permute-start) | collective-permute-done | bytes 589856 | tf_op jit(solution)/shard_map/ppermute | solution.py:12
  171.7 3.4 %collective-permute-start.1 = (bf16[256,1152]{1,0:T(8,128)(2,1)}, bf16[256,1152]{1,0:T(8,128)(2,1)}, u32[]{:S(2)}, u32[]{:S(2)}) collective-permute-start(bf16[256,1152]{1,0:T(8,128)(2,1)} %collective-permute-done), channel_id=1, source_target_pairs={{0,1},{1,2},{2,3},{3,4},{4,5},{5,6},{6,7},{7,8},{8,9},{9,10},{10,1... | collective-permute-start | bytes 1769480 | tf_op jit(solution)/shard_map/ppermute | solution.py:12
  175.1 0.0 collective-permute-done.2
  175.1 2.4 collective-permute-start.3
  177.6 3.2 convolution_add_fusion.3
  180.8 2.3 convolution_add_fusion.1
  183.1 5.0 %collective-permute-done.1 = bf16[256,1152]{1,0:T(8,128)(2,1)} collective-permute-done((bf16[256,1152]{1,0:T(8,128)(2,1)}, bf16[256,1152]{1,0:T(8,128)(2,1)}, u32[]{:S(2)}, u32[]{:S(2)}) %collective-permute-start.1) | collective-permute-done | bytes 589856 | tf_op jit(solution)/shard_map/ppermute | solution.py:12
  188.1 2.6 fusion
  190.6 0.1 concatenate.13
  190.8 2.0 collective-permute-done.3
  192.8 3.1 fusion.1
  195.9 1.5 concatenate.14
  197.4 0.5 pad_maximum_fusion
  197.9 126.1 %all_to_all.10 = bf16[64,4,2304]{2,1,0:T(4,128)(2,1)S(1)} all-to-all(bf16[64,4,2304]{2,1,0:T(4,128)(2,1)S(1)} %pad_maximum_fusion), channel_id=1, replica_groups=mesh['grp'=16,'blk'=64] {'blk'}, dimensions={0} | all-to-all | bytes 2359296 | tf_op jit(solution)/shard_map/all_to_all | solution.py:38
  324.0 0.3 reshape.23
  324.3 0.4 convolution_convert_fusion.1
  324.7 0.9 fusion.76
Async XLA Ops:
  4.9 149.4 %all-to-all-start = ((bf16[64,4,2304]{2,1,0:T(4,128)(2,1)}), bf16[64,4,2304]{2,1,0:T(4,128)(2,1)S(1)}, u32[]{:S(2)}, u32[]{:S(2)}) async-start(bf16[64,4,2304]{2,1,0:T(4,128)(2,1)} %reshape.21), calls=%async_computation | async-start | bytes 2359296 | tf_op jit(solution)/shard_map/all_to_all | solution.py:38
  154.7 17.0 %collective-permute-start = (bf16[256,1152]{1,0:T(8,128)(2,1)S(1)}, bf16[256,1152]{1,0:T(8,128)(2,1)}, u32[]{:S(2)}, u32[]{:S(2)}) collective-permute-start(bf16[256,1152]{1,0:T(8,128)(2,1)S(1)} %get-tuple-element.2), channel_id=1, source_target_pairs={{0,1},{1,2},{2,3},{3,4},{4,5},{5,6},{6,7},{7,8},{8,9},{9,10},{10,1... | collective-permute-start | bytes 1769480 | tf_op jit(solution)/shard_map/ppermute | solution.py:12
  156.6 18.5 %collective-permute-start.2 = (bf16[256,1152]{1,0:T(8,128)(2,1)S(1)}, bf16[256,1152]{1,0:T(8,128)(2,1)}, u32[]{:S(2)}, u32[]{:S(2)}) collective-permute-start(bf16[256,1152]{1,0:T(8,128)(2,1)S(1)} %get-tuple-element.3), channel_id=1, source_target_pairs={{0,1023},{1,0},{2,1},{3,2},{4,3},{5,4},{6,5},{7,6},{8,7},{9,8},{10... | collective-permute-start | bytes 1769480 | tf_op jit(solution)/shard_map/ppermute | solution.py:12
  171.7 16.4 %collective-permute-start.1 = (bf16[256,1152]{1,0:T(8,128)(2,1)}, bf16[256,1152]{1,0:T(8,128)(2,1)}, u32[]{:S(2)}, u32[]{:S(2)}) collective-permute-start(bf16[256,1152]{1,0:T(8,128)(2,1)} %collective-permute-done), channel_id=1, source_target_pairs={{0,1},{1,2},{2,3},{3,4},{4,5},{5,6},{6,7},{7,8},{8,9},{9,10},{10,1... | collective-permute-start | bytes 1769480 | tf_op jit(solution)/shard_map/ppermute | solution.py:12
  175.1 17.6 %collective-permute-start.3 = (bf16[256,1152]{1,0:T(8,128)(2,1)}, bf16[256,1152]{1,0:T(8,128)(2,1)}, u32[]{:S(2)}, u32[]{:S(2)}) collective-permute-start(bf16[256,1152]{1,0:T(8,128)(2,1)} %collective-permute-done.2), channel_id=1, source_target_pairs={{0,1023},{1,0},{2,1},{3,2},{4,3},{5,4},{6,5},{7,6},{8,7},{9,8},{10... | collective-permute-start | bytes 1769480 | tf_op jit(solution)/shard_map/ppermute | solution.py:12

commit v2 on v1

v2 whole, which is shorter than its diff:
```python
import jax
import jax.numpy as jnp
from jax import lax
from jax.sharding import Mesh, PartitionSpec as P

STEPS = 2
GRP, Y_HI, Z = 16, 2, 32
AXES = ("grp", "y_hi", "z_hi", "z_lo")
REGION = ("grp", "y_hi", "z_lo")


def device_at(x, y, core, z):
    return (((x * 2 + y % 2) * 2 + core) * Y_HI + y // 2) * Z + z


def routes():
    in_plane, along_z = [], []
    for g in range(GRP):
        for y_hi in range(Y_HI):
            for z in range(Z):
                column = (g - z + 8 * y_hi) % GRP
                source = (g * Y_HI + y_hi) * Z + z
                via = device_at(column // 4, column % 4, y_hi, z)
                held = device_at(column // 4, column % 4, y_hi, 2 * g + z // GRP)
                in_plane.append((source, via))
                along_z.append((via, held))
    return in_plane, along_z


IN_PLANE, ALONG_Z = routes()
VIA_TO_HELD = dict(ALONG_Z)
TO_REGION = [(source, VIA_TO_HELD[via]) for source, via in IN_PLANE]
FROM_REGION = [(held, source) for source, held in TO_REGION]


def owner_place(position):
    core, chip = position & 1, position >> 1
    x = (chip >> 2) & 3
    y = (chip - x) & 3
    return x, y, core, chip >> 4


def owner_device(owner):
    group, position = owner // 64, owner % 64
    x, y, core, z_lo = owner_place(position)
    return device_at(x, y, core, 2 * group + z_lo)


OWNERS = [owner_device(owner) for owner in range(GRP * Y_HI * Z)]
NEXT = [(OWNERS[i], OWNERS[(i + 1) % len(OWNERS)]) for i in range(len(OWNERS))]
BEFORE = [(b, a) for a, b in NEXT]


def moved(x, route):
    return lax.ppermute(x, AXES, route)


def weight_matrix(picture_batch, caption_batch, scale, offset, matching_label):
    scores = lax.dot_general(
        picture_batch,
        caption_batch,
        (((1,), (1,)), ((), ())),
        preferred_element_type=jnp.float32,
    )
    pair_scores = scale * scores + offset
    return (scale * (jax.nn.sigmoid(pair_scores) - matching_label)).astype(jnp.bfloat16)


def times_rows(weights, rows):
    return jnp.dot(weights, rows, preferred_element_type=jnp.float32)


def rows_of_transpose(weights, rows):
    return lax.dot_general(
        weights, rows, (((0,), (0,)), ((), ())), preferred_element_type=jnp.float32
    )


def swap_blocks(x, devices):
    slots, width = x.shape
    out = lax.all_to_all(
        x.reshape(devices, slots // devices, width),
        REGION,
        split_axis=0,
        concat_axis=0,
        tiled=True,
    )
    return out.reshape(slots, width)


def body(picture_embeds, caption_embeds, holder_position, score_scaling, score_offset_term):
    rows_here = picture_embeds.shape[0]
    devices = lax.axis_size(REGION)
    capacity = 2 * rows_here // devices
    slots = devices * capacity
    scale = score_scaling[0]
    offset = score_offset_term[0]

    position = moved(holder_position, TO_REGION)
    captions_via = moved(caption_embeds, IN_PLANE)
    pictures_via = moved(picture_embeds, IN_PLANE)
    captions_held = moved(captions_via, ALONG_Z)
    pictures_held = moved(pictures_via, ALONG_Z)

    same = position[:, None] == position[None, :]
    order = jnp.arange(rows_here, dtype=jnp.int32)
    rank_in = jnp.sum((same & (order[None, :] < order[:, None])).astype(jnp.int32), axis=1)
    x, y, core, z_lo = owner_place(position)
    owner = (((x * 2 + (y & 1)) * 2 + core) * 2 + (y >> 1)) * 2 + z_lo
    placer = (
        jnp.arange(slots, dtype=jnp.int32)[:, None] == (owner * capacity + rank_in)[None, :]
    ).astype(jnp.bfloat16)

    captions = swap_blocks(times_rows(placer, captions_held).astype(jnp.bfloat16), devices)
    pictures = swap_blocks(times_rows(placer, pictures_held).astype(jnp.bfloat16), devices)

    earlier_captions = [captions]
    later_pictures = [pictures]
    for _ in range(STEPS):
        earlier_captions.append(moved(earlier_captions[-1], NEXT))
        later_pictures.append(moved(later_pictures[-1], BEFORE))

    identity_square = jnp.eye(slots, dtype=jnp.float32)
    own_weights = weight_matrix(pictures, captions, scale, offset, identity_square)
    image_total = times_rows(own_weights, captions)
    text_total = rows_of_transpose(own_weights, pictures)
    zero = jnp.float32(0.0)
    for step in range(1, STEPS + 1):
        weights = weight_matrix(pictures, earlier_captions[step], scale, offset, zero)
        image_total = image_total + times_rows(weights, earlier_captions[step])
    image_back = swap_blocks(image_total.astype(jnp.bfloat16), devices)
    for step in range(1, STEPS + 1):
        weights = weight_matrix(later_pictures[step], captions, scale, offset, zero)
        text_total = text_total + rows_of_transpose(weights, later_pictures[step])
    text_back = swap_blocks(text_total.astype(jnp.bfloat16), devices)

    image_grad = moved(rows_of_transpose(placer, image_back).astype(jnp.bfloat16), FROM_REGION)
    text_grad = moved(rows_of_transpose(placer, text_back).astype(jnp.bfloat16), FROM_REGION)
    return (image_grad, text_grad)


def solution(mesh):
    cut = Mesh(mesh.devices.reshape(GRP, Y_HI, Z // 2, 2), AXES)
    placed = (P(AXES, None), P(AXES, None), P(AXES), P(), P())
    return jax.shard_map(
        body,
        mesh=cut,
        in_specs=placed,
        out_specs=(P(AXES, None), P(AXES, None)),
        check_vma=False,
    )
```

time: 326 us -> 317 us (0.972)
  the two profiles are of different devices: /device:TPU:102 before, /device:TPU:27 now
where the time goes in v2:
time: 317 us; the launch traced here: 316 us
  starting transfers between devices  170 us (54%)
  waiting for transfers between devices  125 us (39%)
  matrix products  11.3 us (4%)
  local copies, waits for them, and re-layouts  7.19 us (2%)
    all_to_all x4, starting transfers between devices, swap_blocks(): lax.all_to_all(x.reshape(devices, slots // devices, width), REGION, split...  112 us
    ppermute x11, waiting for transfers between devices, moved(): return lax.ppermute(x, AXES, route)  96.2 us
    ppermute x11, starting transfers between devices, moved(): return lax.ppermute(x, AXES, route)  58.1 us
    all_to_all x4, waiting for transfers between devices, swap_blocks(): lax.all_to_all(x.reshape(devices, slots // devices, width), REGION, split...  29.2 us
  transfers between devices with their start and end apart: 15, of which 11 were waited for; matrix products, arithmetic and copies ran while one was open for 4% of the time, Pallas kernels for 0%

profile of v2, /device:TPU:27, one launch (start us, length us, event | category | flops | bytes accessed | tf_op | source)
XLA Modules:
  0.0 316.0 jit_solution(7574325323785077443)
XLA Ops:
  0.6 3.8 %collective-permute-start.1 = (bf16[128,1152]{1,0:T(8,128)(2,1)}, bf16[128,1152]{1,0:T(8,128)(2,1)S(1)}, u32[]{:S(2)}, u32[]{:S(2)}) collective-permute-start(bf16[128,1152]{1,0:T(8,128)(2,1)} %param.5), channel_id=1, source_target_pairs={{0,0},{1,929},{2,802},{3,899},{4,772},{5,677},{6,550},{7,647},{8,5... | collective-permute-start | bytes 884744 | tf_op jit(solution)/shard_map/ppermute | solution.py:55
  4.4 25.7 %collective-permute-start = (s32[128]{0:T(128)}, s32[128]{0:T(128)S(1)}, u32[]{:S(2)}, u32[]{:S(2)}) collective-permute-start(s32[128]{0:T(128)} %param.7), channel_id=1, source_target_pairs={{0,0},{1,928},{2,800},{3,896},{4,768},{5,672},{6,544},{7,640},{8,5... | collective-permute-start | bytes 1544 | tf_op jit(solution)/shard_map/ppermute | solution.py:55
  30.1 0.0 collective-permute-done.1
  30.1 5.2 %collective-permute-start.2 = (bf16[128,1152]{1,0:T(8,128)(2,1)S(1)}, bf16[128,1152]{1,0:T(8,128)(2,1)S(1)}, u32[]{:S(2)}, u32[]{:S(2)}) collective-permute-start(bf16[128,1152]{1,0:T(8,128)(2,1)S(1)} %collective-permute-done.1), channel_id=1, source_target_pairs={{0,0},{929,928},{802,800},{899,896},{772,768},{677,672},{550,544},... | collective-permute-start | bytes 884744 | tf_op jit(solution)/shard_map/ppermute | solution.py:55
  35.3 0.0 collective-permute-done
  35.3 0.2 convert_reduce_fusion
  35.5 3.5 %collective-permute-done.2 = bf16[128,1152]{1,0:T(8,128)(2,1)S(1)} collective-permute-done((bf16[128,1152]{1,0:T(8,128)(2,1)S(1)}, bf16[128,1152]{1,0:T(8,128)(2,1)S(1)}, u32[]{:S(2)}, u32[]{:S(2)}) %collective-permute-start.2) | collective-permute-done | bytes 294944 | tf_op jit(solution)/shard_map/ppermute | solution.py:55
  39.0 0.3 convolution_convert_fusion.1
  39.3 0.0 copy-start.2
  39.3 1.0 reshape.31
  40.3 47.1 %all-to-all-start = ((bf16[64,4,1152]{2,1,0:T(4,128)(2,1)}), bf16[64,4,1152]{2,1,0:T(4,128)(2,1)S(1)}, u32[]{:S(2)}, u32[]{:S(2)}) async-start(bf16[64,4,1152]{2,1,0:T(4,128)(2,1)} %reshape.31), calls=%async_computation | async-start | bytes 1179648 | tf_op jit(solution)/shard_map/all_to_all | solution.py:81
  87.4 0.0 copy-done.2
  87.4 3.9 %collective-permute-start.3 = (bf16[128,1152]{1,0:T(8,128)(2,1)S(1)}, bf16[128,1152]{1,0:T(8,128)(2,1)S(1)}, u32[]{:S(2)}, u32[]{:S(2)}) collective-permute-start(bf16[128,1152]{1,0:T(8,128)(2,1)S(1)} %copy-done.2), channel_id=1, source_target_pairs={{0,0},{1,929},{2,802},{3,899},{4,772},{5,677},{6,550},{7,647},{8,5... | collective-permute-start | bytes 884744 | tf_op jit(solution)/shard_map/ppermute | solution.py:55
  91.4 11.0 %collective-permute-done.3 = bf16[128,1152]{1,0:T(8,128)(2,1)S(1)} collective-permute-done((bf16[128,1152]{1,0:T(8,128)(2,1)S(1)}, bf16[128,1152]{1,0:T(8,128)(2,1)S(1)}, u32[]{:S(2)}, u32[]{:S(2)}) %collective-permute-start.3) | collective-permute-done | bytes 294944 | tf_op jit(solution)/shard_map/ppermute | solution.py:55
  102.4 1.9 collective-permute-start.4
  104.4 5.5 %collective-permute-done.4 = bf16[128,1152]{1,0:T(8,128)(2,1)S(1)} collective-permute-done((bf16[128,1152]{1,0:T(8,128)(2,1)S(1)}, bf16[128,1152]{1,0:T(8,128)(2,1)S(1)}, u32[]{:S(2)}, u32[]{:S(2)}) %collective-permute-start.4) | collective-permute-done | bytes 294944 | tf_op jit(solution)/shard_map/ppermute | solution.py:55
  109.9 0.3 convolution_convert_fusion
  110.2 1.0 reshape.33
  111.1 0.0 all-to-all-done
  111.1 46.5 %all-to-all-start.1 = ((bf16[64,4,1152]{2,1,0:T(4,128)(2,1)}), bf16[64,4,1152]{2,1,0:T(4,128)(2,1)S(1)}, u32[]{:S(2)}, u32[]{:S(2)}) async-start(bf16[64,4,1152]{2,1,0:T(4,128)(2,1)} %reshape.33), calls=%async_computation.1 | async-start | bytes 1179648 | tf_op jit(solution)/shard_map/all_to_all | solution.py:81
  157.6 0.1 reshape.32
  157.8 2.3 collective-permute-start.8
  161.3 6.3 %all-to-all-done.1 = bf16[64,4,1152]{2,1,0:T(4,128)(2,1)S(1)} async-done(((bf16[64,4,1152]{2,1,0:T(4,128)(2,1)}), bf16[64,4,1152]{2,1,0:T(4,128)(2,1)S(1)}, u32[]{:S(2)}, u32[]{:S(2)}) %all-to-all-start.1) | async-done | bytes 589856 | tf_op jit(solution)/shard_map/all_to_all | solution.py:81
  167.6 0.1 reshape.34
  167.8 0.4 fusion.33
  168.2 0.0 copy-start
  168.2 4.1 %collective-permute-done.8 = bf16[256,1152]{1,0:T(8,128)(2,1)} collective-permute-done((bf16[256,1152]{1,0:T(8,128)(2,1)S(1)}, bf16[256,1152]{1,0:T(8,128)(2,1)}, u32[]{:S(2)}, u32[]{:S(2)}) %collective-permute-start.8) | collective-permute-done | bytes 589856 | tf_op jit(solution)/shard_map/ppermute | solution.py:55
  172.2 1.9 collective-permute-start.9
  174.2 0.4 fusion.61
  174.5 0.0 copy-done
  174.6 2.3 convolution_add_fusion.1
  176.8 8.1 %collective-permute-done.9 = bf16[256,1152]{1,0:T(8,128)(2,1)} collective-permute-done((bf16[256,1152]{1,0:T(8,128)(2,1)}, bf16[256,1152]{1,0:T(8,128)(2,1)}, u32[]{:S(2)}, u32[]{:S(2)}) %collective-permute-start.9) | collective-permute-done | bytes 589856 | tf_op jit(solution)/shard_map/ppermute | solution.py:55
  185.0 2.3 fusion.1
  187.3 0.0 copy-start.1
  187.3 1.0 reshape.37
  188.3 8.2 %all-to-all-start.3 = ((bf16[64,4,1152]{2,1,0:T(4,128)(2,1)}), bf16[64,4,1152]{2,1,0:T(4,128)(2,1)}, u32[]{:S(2)}, u32[]{:S(2)}) async-start(bf16[64,4,1152]{2,1,0:T(4,128)(2,1)} %reshape.37), calls=%async_computation.3 | async-start | bytes 1179648 | tf_op jit(solution)/shard_map/all_to_all | solution.py:81
  196.5 2.4 collective-permute-start.5
  198.8 10.9 %collective-permute-done.5 = bf16[256,1152]{1,0:T(8,128)(2,1)} collective-permute-done((bf16[256,1152]{1,0:T(8,128)(2,1)S(1)}, bf16[256,1152]{1,0:T(8,128)(2,1)}, u32[]{:S(2)}, u32[]{:S(2)}) %collective-permute-start.5) | collective-permute-done | bytes 589856 | tf_op jit(solution)/shard_map/ppermute | solution.py:55
  209.7 5.7 %collective-permute-start.6 = (bf16[256,1152]{1,0:T(8,128)(2,1)}, bf16[256,1152]{1,0:T(8,128)(2,1)}, u32[]{:S(2)}, u32[]{:S(2)}) collective-permute-start(bf16[256,1152]{1,0:T(8,128)(2,1)} %collective-permute-done.5), channel_id=1, source_target_pairs={{0,64},{64,128},{128,192},{192,32},{32,96},{96,160},{160,224},{224... | collective-permute-start | bytes 1769480 | tf_op jit(solution)/shard_map/ppermute | solution.py:55
  215.4 0.0 copy-done.1
  215.4 0.3 fusion.60
  215.8 2.2 convolution_add_fusion.3
  218.0 4.6 %collective-permute-done.6 = bf16[256,1152]{1,0:T(8,128)(2,1)} collective-permute-done((bf16[256,1152]{1,0:T(8,128)(2,1)}, bf16[256,1152]{1,0:T(8,128)(2,1)}, u32[]{:S(2)}, u32[]{:S(2)}) %collective-permute-start.6) | collective-permute-done | bytes 589856 | tf_op jit(solution)/shard_map/ppermute | solution.py:55
  222.6 2.3 fusion
  224.8 1.0 reshape.35
  225.8 0.0 all-to-all-done.3
  225.8 9.8 %all-to-all-start.2 = ((bf16[64,4,1152]{2,1,0:T(4,128)(2,1)}), bf16[64,4,1152]{2,1,0:T(4,128)(2,1)S(1)}, u32[]{:S(2)}, u32[]{:S(2)}) async-start(bf16[64,4,1152]{2,1,0:T(4,128)(2,1)} %reshape.35), calls=%async_computation.2 | async-start | bytes 1179648 | tf_op jit(solution)/shard_map/all_to_all | solution.py:81
  235.6 1.5 reshape.38
  237.0 0.3 convolution_convert_fusion.2
  237.3 3.5 %collective-permute-start.10 = (bf16[128,1152]{1,0:T(8,128)(2,1)S(1)}, bf16[128,1152]{1,0:T(8,128)(2,1)S(1)}, u32[]{:S(2)}, u32[]{:S(2)}) collective-permute-start(bf16[128,1152]{1,0:T(8,128)(2,1)S(1)} %convolution_convert_fusion.2), channel_id=1, source_target_pairs={{0,0},{928,1},{800,2},{896,3},{768,4},{672,5},{544,6},{640,7},{512... | collective-permute-start | bytes 884744 | tf_op jit(solution)/shard_map/ppermute | solution.py:55
  240.8 22.9 %all-to-all-done.2 = bf16[64,4,1152]{2,1,0:T(4,128)(2,1)S(1)} async-done(((bf16[64,4,1152]{2,1,0:T(4,128)(2,1)}), bf16[64,4,1152]{2,1,0:T(4,128)(2,1)S(1)}, u32[]{:S(2)}, u32[]{:S(2)}) %all-to-all-start.2) | async-done | bytes 589856 | tf_op jit(solution)/shard_map/all_to_all | solution.py:81
  263.7 0.1 reshape.36
  263.8 0.3 convolution_convert_fusion.3
  264.1 1.9 collective-permute-start.7
  266.1 10.3 %collective-permute-done.10 = bf16[128,1152]{1,0:T(8,128)(2,1)S(1)} collective-permute-done((bf16[128,1152]{1,0:T(8,128)(2,1)S(1)}, bf16[128,1152]{1,0:T(8,128)(2,1)S(1)}, u32[]{:S(2)}, u32[]{:S(2)}) %collective-permute-start.10) | collective-permute-done | bytes 294944 | tf_op jit(solution)/shard_map/ppermute | solution.py:55
  276.4 38.2 %collective-permute-done.7 = bf16[128,1152]{1,0:T(8,128)(2,1)S(1)} collective-permute-done((bf16[128,1152]{1,0:T(8,128)(2,1)S(1)}, bf16[128,1152]{1,0:T(8,128)(2,1)S(1)}, u32[]{:S(2)}, u32[]{:S(2)}) %collective-permute-start.7) | collective-permute-done | bytes 294944 | tf_op jit(solution)/shard_map/ppermute | solution.py:55
  314.5 0.7 copy.11
  315.3 0.7 copy.12
  (1 shorter events, 0.0 us)
Async XLA Ops:
  0.6 29.5 %collective-permute-start.1 = (bf16[128,1152]{1,0:T(8,128)(2,1)}, bf16[128,1152]{1,0:T(8,128)(2,1)S(1)}, u32[]{:S(2)}, u32[]{:S(2)}) collective-permute-start(bf16[128,1152]{1,0:T(8,128)(2,1)} %param.5), channel_id=1, source_target_pairs={{0,0},{1,929},{2,802},{3,899},{4,772},{5,677},{6,550},{7,647},{8,5... | collective-permute-start | bytes 884744 | tf_op jit(solution)/shard_map/ppermute | solution.py:55
  4.4 30.9 %collective-permute-start = (s32[128]{0:T(128)}, s32[128]{0:T(128)S(1)}, u32[]{:S(2)}, u32[]{:S(2)}) collective-permute-start(s32[128]{0:T(128)} %param.7), channel_id=1, source_target_pairs={{0,0},{1,928},{2,800},{3,896},{4,768},{5,672},{6,544},{7,640},{8,5... | collective-permute-start | bytes 1544 | tf_op jit(solution)/shard_map/ppermute | solution.py:55
  30.1 8.9 %collective-permute-start.2 = (bf16[128,1152]{1,0:T(8,128)(2,1)S(1)}, bf16[128,1152]{1,0:T(8,128)(2,1)S(1)}, u32[]{:S(2)}, u32[]{:S(2)}) collective-permute-start(bf16[128,1152]{1,0:T(8,128)(2,1)S(1)} %collective-permute-done.1), channel_id=1, source_target_pairs={{0,0},{929,928},{802,800},{899,896},{772,768},{677,672},{550,544},... | collective-permute-start | bytes 884744 | tf_op jit(solution)/shard_map/ppermute | solution.py:55
  39.3 48.1 %copy-start.2 = (bf16[128,1152]{1,0:T(8,128)(2,1)S(1)}, bf16[128,1152]{1,0:T(8,128)(2,1)}, u32[]{:S(2)}) copy-start(bf16[128,1152]{1,0:T(8,128)(2,1)} %param.6) | copy-start | bytes 884740
  40.3 70.9 %all-to-all-start = ((bf16[64,4,1152]{2,1,0:T(4,128)(2,1)}), bf16[64,4,1152]{2,1,0:T(4,128)(2,1)S(1)}, u32[]{:S(2)}, u32[]{:S(2)}) async-start(bf16[64,4,1152]{2,1,0:T(4,128)(2,1)} %reshape.31), calls=%async_computation | async-start | bytes 1179648 | tf_op jit(solution)/shard_map/all_to_all | solution.py:81
  87.4 15.0 %collective-permute-start.3 = (bf16[128,1152]{1,0:T(8,128)(2,1)S(1)}, bf16[128,1152]{1,0:T(8,128)(2,1)S(1)}, u32[]{:S(2)}, u32[]{:S(2)}) collective-permute-start(bf16[128,1152]{1,0:T(8,128)(2,1)S(1)} %copy-done.2), channel_id=1, source_target_pairs={{0,0},{1,929},{2,802},{3,899},{4,772},{5,677},{6,550},{7,647},{8,5... | collective-permute-start | bytes 884744 | tf_op jit(solution)/shard_map/ppermute | solution.py:55
  102.4 7.5 %collective-permute-start.4 = (bf16[128,1152]{1,0:T(8,128)(2,1)S(1)}, bf16[128,1152]{1,0:T(8,128)(2,1)S(1)}, u32[]{:S(2)}, u32[]{:S(2)}) collective-permute-start(bf16[128,1152]{1,0:T(8,128)(2,1)S(1)} %collective-permute-done.3), channel_id=1, source_target_pairs={{0,0},{929,928},{802,800},{899,896},{772,768},{677,672},{550,544},... | collective-permute-start | bytes 884744 | tf_op jit(solution)/shard_map/ppermute | solution.py:55
  111.1 56.5 %all-to-all-start.1 = ((bf16[64,4,1152]{2,1,0:T(4,128)(2,1)}), bf16[64,4,1152]{2,1,0:T(4,128)(2,1)S(1)}, u32[]{:S(2)}, u32[]{:S(2)}) async-start(bf16[64,4,1152]{2,1,0:T(4,128)(2,1)} %reshape.33), calls=%async_computation.1 | async-start | bytes 1179648 | tf_op jit(solution)/shard_map/all_to_all | solution.py:81
  157.8 14.5 %collective-permute-start.8 = (bf16[256,1152]{1,0:T(8,128)(2,1)S(1)}, bf16[256,1152]{1,0:T(8,128)(2,1)}, u32[]{:S(2)}, u32[]{:S(2)}) collective-permute-start(bf16[256,1152]{1,0:T(8,128)(2,1)S(1)} %reshape.32), channel_id=1, source_target_pairs={{64,0},{128,64},{192,128},{32,192},{96,32},{160,96},{224,160},{416... | collective-permute-start | bytes 1769480 | tf_op jit(solution)/shard_map/ppermute | solution.py:55
  168.2 6.4 %copy-start = (bf16[256,256]{1,0:T(8,128)(2,1)}, bf16[256,256]{1,0:T(8,128)(2,1)S(1)}, u32[]{:S(2)}) copy-start(bf16[256,256]{1,0:T(8,128)(2,1)S(1)} %fusion.33) | copy-start | bytes 393220
  172.2 12.7 %collective-permute-start.9 = (bf16[256,1152]{1,0:T(8,128)(2,1)}, bf16[256,1152]{1,0:T(8,128)(2,1)}, u32[]{:S(2)}, u32[]{:S(2)}) collective-permute-start(bf16[256,1152]{1,0:T(8,128)(2,1)} %collective-permute-done.8), channel_id=1, source_target_pairs={{64,0},{128,64},{192,128},{32,192},{96,32},{160,96},{224,160},{416... | collective-permute-start | bytes 1769480 | tf_op jit(solution)/shard_map/ppermute | solution.py:55
  187.3 28.1 %copy-start.1 = (bf16[256,256]{1,0:T(8,128)(2,1)S(1)}, bf16[256,256]{1,0:T(8,128)(2,1)}, u32[]{:S(2)}) copy-start(bf16[256,256]{1,0:T(8,128)(2,1)} %copy-done) | copy-start | bytes 393220
  188.3 37.5 %all-to-all-start.3 = ((bf16[64,4,1152]{2,1,0:T(4,128)(2,1)}), bf16[64,4,1152]{2,1,0:T(4,128)(2,1)}, u32[]{:S(2)}, u32[]{:S(2)}) async-start(bf16[64,4,1152]{2,1,0:T(4,128)(2,1)} %reshape.37), calls=%async_computation.3 | async-start | bytes 1179648 | tf_op jit(solution)/shard_map/all_to_all | solution.py:81
  196.5 13.3 %collective-permute-start.5 = (bf16[256,1152]{1,0:T(8,128)(2,1)S(1)}, bf16[256,1152]{1,0:T(8,128)(2,1)}, u32[]{:S(2)}, u32[]{:S(2)}) collective-permute-start(bf16[256,1152]{1,0:T(8,128)(2,1)S(1)} %reshape.34), channel_id=1, source_target_pairs={{0,64},{64,128},{128,192},{192,32},{32,96},{96,160},{160,224},{224... | collective-permute-start | bytes 1769480 | tf_op jit(solution)/shard_map/ppermute | solution.py:55
  209.7 12.8 %collective-permute-start.6 = (bf16[256,1152]{1,0:T(8,128)(2,1)}, bf16[256,1152]{1,0:T(8,128)(2,1)}, u32[]{:S(2)}, u32[]{:S(2)}) collective-permute-start(bf16[256,1152]{1,0:T(8,128)(2,1)} %collective-permute-done.5), channel_id=1, source_target_pairs={{0,64},{64,128},{128,192},{192,32},{32,96},{96,160},{160,224},{224... | collective-permute-start | bytes 1769480 | tf_op jit(solution)/shard_map/ppermute | solution.py:55
  225.8 37.9 %all-to-all-start.2 = ((bf16[64,4,1152]{2,1,0:T(4,128)(2,1)}), bf16[64,4,1152]{2,1,0:T(4,128)(2,1)S(1)}, u32[]{:S(2)}, u32[]{:S(2)}) async-start(bf16[64,4,1152]{2,1,0:T(4,128)(2,1)} %reshape.35), calls=%async_computation.2 | async-start | bytes 1179648 | tf_op jit(solution)/shard_map/all_to_all | solution.py:81
  237.3 39.0 %collective-permute-start.10 = (bf16[128,1152]{1,0:T(8,128)(2,1)S(1)}, bf16[128,1152]{1,0:T(8,128)(2,1)S(1)}, u32[]{:S(2)}, u32[]{:S(2)}) collective-permute-start(bf16[128,1152]{1,0:T(8,128)(2,1)S(1)} %convolution_convert_fusion.2), channel_id=1, source_target_pairs={{0,0},{928,1},{800,2},{896,3},{768,4},{672,5},{544,6},{640,7},{512... | collective-permute-start | bytes 884744 | tf_op jit(solution)/shard_map/ppermute | solution.py:55
  264.1 50.4 %collective-permute-start.7 = (bf16[128,1152]{1,0:T(8,128)(2,1)S(1)}, bf16[128,1152]{1,0:T(8,128)(2,1)S(1)}, u32[]{:S(2)}, u32[]{:S(2)}) collective-permute-start(bf16[128,1152]{1,0:T(8,128)(2,1)S(1)} %convolution_convert_fusion.3), channel_id=1, source_target_pairs={{0,0},{928,1},{800,2},{896,3},{768,4},{672,5},{544,6},{640,7},{512... | collective-permute-start | bytes 884744 | tf_op jit(solution)/shard_map/ppermute | solution.py:55

commit v3 on v2

--- a/solution.py
+++ b/solution.py
@@ -18,7 +18,7 @@
     for g in range(GRP):
         for y_hi in range(Y_HI):
             for z in range(Z):
-                column = (g - z + 8 * y_hi) % GRP
+                column = (3 * g - 3 * z + 8 * y_hi) % GRP
                 source = (g * Y_HI + y_hi) * Z + z
                 via = device_at(column // 4, column % 4, y_hi, z)
                 held = device_at(column // 4, column % 4, y_hi, 2 * g + z // GRP)
@@ -89,7 +89,7 @@
 
 
 def body(picture_embeds, caption_embeds, holder_position, score_scaling, score_offset_term):
-    rows_here = picture_embeds.shape[0]
+    rows_here, width = picture_embeds.shape
     devices = lax.axis_size(REGION)
     capacity = 2 * rows_here // devices
     slots = devices * capacity
@@ -98,6 +98,9 @@
 
     position = moved(holder_position, TO_REGION)
     captions_via = moved(caption_embeds, IN_PLANE)
+    captions_via, picture_embeds, position = lax.optimization_barrier(
+        (captions_via, picture_embeds, position)
+    )
     pictures_via = moved(picture_embeds, IN_PLANE)
     captions_held = moved(captions_via, ALONG_Z)
     pictures_held = moved(pictures_via, ALONG_Z)
@@ -111,8 +114,10 @@
         jnp.arange(slots, dtype=jnp.int32)[:, None] == (owner * capacity + rank_in)[None, :]
     ).astype(jnp.bfloat16)
 
-    captions = swap_blocks(times_rows(placer, captions_held).astype(jnp.bfloat16), devices)
-    pictures = swap_blocks(times_rows(placer, pictures_held).astype(jnp.bfloat16), devices)
+    placed = [times_rows(placer, held) for held in (pictures_held, captions_held)]
+    received = swap_blocks(jnp.concatenate(placed, axis=1).astype(jnp.bfloat16), devices)
+    pictures = received[:, :width]
+    captions = received[:, width:]
 
     earlier_captions = [captions]
     later_pictures = [pictures]
@@ -128,13 +133,15 @@
     for step in range(1, STEPS + 1):
         weights = weight_matrix(pictures, earlier_captions[step], scale, offset, zero)
         image_total = image_total + times_rows(weights, earlier_captions[step])
-    image_back = swap_blocks(image_total.astype(jnp.bfloat16), devices)
+    image_done = image_total.astype(jnp.bfloat16)
+    image_done, *later_pictures = lax.optimization_barrier((image_done, *later_pictures))
+    image_back = swap_blocks(image_done, devices)
+    image_grad = moved(rows_of_transpose(placer, image_back).astype(jnp.bfloat16), FROM_REGION)
+
     for step in range(1, STEPS + 1):
         weights = weight_matrix(later_pictures[step], captions, scale, offset, zero)
         text_total = text_total + rows_of_transpose(weights, later_pictures[step])
     text_back = swap_blocks(text_total.astype(jnp.bfloat16), devices)
-
-    image_grad = moved(rows_of_transpose(placer, image_back).astype(jnp.bfloat16), FROM_REGION)
     text_grad = moved(rows_of_transpose(placer, text_back).astype(jnp.bfloat16), FROM_REGION)
     return (image_grad, text_grad)
 

time: 317 us -> 290 us (0.915)
  the two profiles are of different devices: /device:TPU:27 before, /device:TPU:3 now
where the time goes in v3:
time: 290 us; the launch traced here: 289 us
  starting transfers between devices  162 us (56%)
  waiting for transfers between devices  61 us (21%)
  blocking collectives  45.2 us (16%)
  matrix products  13.5 us (5%)
  local copies, waits for them, and re-layouts  4.29 us (1%)
    ppermute x11, starting transfers between devices, moved(): return lax.ppermute(x, AXES, route)  134 us
    ppermute x11, waiting for transfers between devices, moved(): return lax.ppermute(x, AXES, route)  51.2 us
    all_to_all x1, blocking collectives, swap_blocks(): lax.all_to_all(x.reshape(devices, slots // devices, width), REGION, split...  45.2 us
    all_to_all x2, starting transfers between devices, swap_blocks(): lax.all_to_all(x.reshape(devices, slots // devices, width), REGION, split...  27.9 us
    all_to_all x2, waiting for transfers between devices, swap_blocks(): lax.all_to_all(x.reshape(devices, slots // devices, width), REGION, split...  9.8 us
    dot_general x5, matrix products, times_rows(): return jnp.dot(weights, rows, preferred_element_type=jnp.float32)  7.57 us
  transfers between devices with their start and end apart: 13, of which 9 were waited for; matrix products, arithmetic and copies ran while one was open for 4% of the time, Pallas kernels for 0%

profile of v3, /device:TPU:3, one launch (start us, length us, event | category | flops | bytes accessed | tf_op | source)
XLA Modules:
  0.0 289.1 jit_solution(9727384178916710723)
XLA Ops:
  0.6 6.8 %collective-permute-start = (bf16[128,1152]{1,0:T(8,128)(2,1)}, bf16[128,1152]{1,0:T(8,128)(2,1)S(1)}, u32[]{:S(2)}, u32[]{:S(2)}) collective-permute-start(bf16[128,1152]{1,0:T(8,128)(2,1)} %param.6), channel_id=1, source_target_pairs={{0,0},{1,897},{2,546},{3,419},{4,260},{5,133},{6,806},{7,679},{8,5... | collective-permute-start | bytes 884744 | tf_op jit(solution)/shard_map/ppermute | solution.py:55
  7.4 18.4 %collective-permute-start.1 = (s32[128]{0:T(128)}, s32[128]{0:T(128)S(1)}, u32[]{:S(2)}, u32[]{:S(2)}) collective-permute-start(s32[128]{0:T(128)} %param.7), channel_id=1, source_target_pairs={{0,0},{1,896},{2,544},{3,416},{4,256},{5,128},{6,800},{7,672},{8,5... | collective-permute-start | bytes 1544 | tf_op jit(solution)/shard_map/ppermute | solution.py:55
  25.8 4.1 %collective-permute-done.1 = s32[128]{0:T(128)S(1)} collective-permute-done((s32[128]{0:T(128)}, s32[128]{0:T(128)S(1)}, u32[]{:S(2)}, u32[]{:S(2)}) %collective-permute-start.1) | collective-permute-done | bytes 544 | tf_op jit(solution)/shard_map/ppermute | solution.py:55
  29.8 0.0 collective-permute-done
  29.8 5.7 %collective-permute-start.2 = (bf16[128,1152]{1,0:T(8,128)(2,1)}, bf16[128,1152]{1,0:T(8,128)(2,1)S(1)}, u32[]{:S(2)}, u32[]{:S(2)}) collective-permute-start(bf16[128,1152]{1,0:T(8,128)(2,1)} %param.5), channel_id=1, source_target_pairs={{0,0},{1,897},{2,546},{3,419},{4,260},{5,133},{6,806},{7,679},{8,5... | collective-permute-start | bytes 884744 | tf_op jit(solution)/shard_map/ppermute | solution.py:55
  35.5 3.8 %collective-permute-start.4 = (bf16[128,1152]{1,0:T(8,128)(2,1)S(1)}, bf16[128,1152]{1,0:T(8,128)(2,1)S(1)}, u32[]{:S(2)}, u32[]{:S(2)}) collective-permute-start(bf16[128,1152]{1,0:T(8,128)(2,1)S(1)} %collective-permute-done), channel_id=1, source_target_pairs={{0,0},{897,896},{546,544},{419,416},{260,256},{133,128},{806,800},... | collective-permute-start | bytes 884744 | tf_op jit(solution)/shard_map/ppermute | solution.py:55
  39.3 0.2 convert_reduce_fusion
  39.5 6.7 %collective-permute-done.2 = bf16[128,1152]{1,0:T(8,128)(2,1)S(1)} collective-permute-done((bf16[128,1152]{1,0:T(8,128)(2,1)}, bf16[128,1152]{1,0:T(8,128)(2,1)S(1)}, u32[]{:S(2)}, u32[]{:S(2)}) %collective-permute-start.2) | collective-permute-done | bytes 294944 | tf_op jit(solution)/shard_map/ppermute | solution.py:55
  46.2 24.4 %collective-permute-start.3 = (bf16[128,1152]{1,0:T(8,128)(2,1)S(1)}, bf16[128,1152]{1,0:T(8,128)(2,1)S(1)}, u32[]{:S(2)}, u32[]{:S(2)}) collective-permute-start(bf16[128,1152]{1,0:T(8,128)(2,1)S(1)} %collective-permute-done.2), channel_id=1, source_target_pairs={{0,0},{897,896},{546,544},{419,416},{260,256},{133,128},{806,800},... | collective-permute-start | bytes 884744 | tf_op jit(solution)/shard_map/ppermute | solution.py:55
  70.6 0.0 collective-permute-done.4
  70.6 0.3 convolution_convert_fusion
  71.0 0.1 concatenate.10
  71.1 18.3 %collective-permute-done.3 = bf16[128,1152]{1,0:T(8,128)(2,1)S(1)} collective-permute-done((bf16[128,1152]{1,0:T(8,128)(2,1)S(1)}, bf16[128,1152]{1,0:T(8,128)(2,1)S(1)}, u32[]{:S(2)}, u32[]{:S(2)}) %collective-permute-start.3) | collective-permute-done | bytes 294944 | tf_op jit(solution)/shard_map/ppermute | solution.py:55
  89.4 0.3 convolution_convert_fusion.1
  89.7 0.1 concatenate.9
  89.9 0.5 pad_maximum_fusion
  90.4 45.2 %all_to_all.15 = bf16[64,4,2304]{2,1,0:T(4,128)(2,1)S(1)} all-to-all(bf16[64,4,2304]{2,1,0:T(4,128)(2,1)S(1)} %pad_maximum_fusion), channel_id=1, replica_groups=mesh['grp'=16,'y_hi'=2,'z_hi'=16,'z_lo'=2] {'grp','y_hi','z_lo'}, dimensions={0} | all-to-all | bytes 2359296 | tf_op jit(solution)/shard_map/all_to_all | solution.py:81
  135.6 0.3 reshape.27
  135.9 0.1 fusion.74
  136.0 2.8 collective-permute-start.5
  140.1 1.9 collective-permute-start.7
  142.0 0.4 fusion.33
  142.4 0.3 fusion.64
  142.8 2.8 collective-permute-done.5
  145.6 4.5 %collective-permute-start.6 = (bf16[256,1152]{1,0:T(8,128)(2,1)}, bf16[256,1152]{1,0:T(8,128)(2,1)}, u32[]{:S(2)}, u32[]{:S(2)}) collective-permute-start(bf16[256,1152]{1,0:T(8,128)(2,1)} %collective-permute-done.5), channel_id=1, source_target_pairs={{0,64},{64,128},{128,192},{192,32},{32,96},{96,160},{160,224},{224... | collective-permute-start | bytes 1769480 | tf_op jit(solution)/shard_map/ppermute | solution.py:55
  150.1 0.4 fusion.67
  150.4 0.9 collective-permute-done.7
  151.4 2.5 collective-permute-start.8
  153.9 3.2 %convolution_add_fusion.3 = f32[256,1152]{1,0:T(8,128)} fusion(f32[256,1152]{1,0:T(8,128)S(1)} %fusion.64, bf16[256,1152]{1,0:T(8,128)(2,1)} %collective-permute-done.5, f32[]{:T(128)} %bitcast.25, f32[]{:T(128)} %bitcast.18, bf16[256,2304]{1,0:T(8,128)(2,1)S(1)} %reshape.27), kind=kOutput, calls=%fused_computation.3 | convolution fusion | flops 302743552 | bytes 4129792 | tf_op jit(solution)/shard_map/dot_general | solution.py:70
  157.1 0.1 collective-permute-done.6
  157.2 3.4 %fusion = bf16[256,1152]{1,0:T(8,128)(2,1)} fusion(f32[256,1152]{1,0:T(8,128)} %convolution_add_fusion.3, bf16[256,1152]{1,0:T(8,128)(2,1)} %collective-permute-done.6, f32[]{:T(128)} %bitcast.24, f32[]{:T(128)} %bitcast.16, bf16[256,2304]{1,0:T(8,128)(2,1)S(1)} %reshape.27), kind=kOutput, calls=%fused_computation.4 | convolution fusion | flops 303038464 | bytes 3539968 | tf_op jit(solution)/shard_map/dot_general | solution.py:70
  160.6 2.3 collective-permute-done.8
  162.9 2.3 convolution_add_fusion.1
  165.2 2.3 fusion.1
  167.5 0.0 copy-start
  167.5 1.0 reshape.30
  168.5 21.1 %all-to-all-start.2 = ((bf16[64,4,1152]{2,1,0:T(4,128)(2,1)}), bf16[64,4,1152]{2,1,0:T(4,128)(2,1)S(1)}, u32[]{:S(2)}, u32[]{:S(2)}) async-start(bf16[64,4,1152]{2,1,0:T(4,128)(2,1)} %reshape.30), calls=%async_computation.2 | async-start | bytes 1179648 | tf_op jit(solution)/shard_map/all_to_all | solution.py:81
  189.6 0.0 copy-done
  189.6 1.0 reshape.28
  190.5 9.8 %all-to-all-done.2 = bf16[64,4,1152]{2,1,0:T(4,128)(2,1)S(1)} async-done(((bf16[64,4,1152]{2,1,0:T(4,128)(2,1)}), bf16[64,4,1152]{2,1,0:T(4,128)(2,1)S(1)}, u32[]{:S(2)}, u32[]{:S(2)}) %all-to-all-start.2) | async-done | bytes 589856 | tf_op jit(solution)/shard_map/all_to_all | solution.py:81
  200.3 6.8 %all-to-all-start.1 = ((bf16[64,4,1152]{2,1,0:T(4,128)(2,1)}), bf16[64,4,1152]{2,1,0:T(4,128)(2,1)S(1)}, u32[]{:S(2)}, u32[]{:S(2)}) async-start(bf16[64,4,1152]{2,1,0:T(4,128)(2,1)} %reshape.28), calls=%async_computation.1 | async-start | bytes 1179648 | tf_op jit(solution)/shard_map/all_to_all | solution.py:81
  207.1 0.1 reshape.31
  207.3 0.3 convolution_convert_fusion.2
  207.6 18.2 %collective-permute-start.10 = (bf16[128,1152]{1,0:T(8,128)(2,1)S(1)}, bf16[128,1152]{1,0:T(8,128)(2,1)S(1)}, u32[]{:S(2)}, u32[]{:S(2)}) collective-permute-start(bf16[128,1152]{1,0:T(8,128)(2,1)S(1)} %convolution_convert_fusion.2), channel_id=1, source_target_pairs={{0,0},{896,1},{544,2},{416,3},{256,4},{128,5},{800,6},{672,7},{512... | collective-permute-start | bytes 884744 | tf_op jit(solution)/shard_map/ppermute | solution.py:55
  225.8 0.0 all-to-all-done.1
  225.8 0.1 reshape.29
  225.9 0.3 convolution_convert_fusion.3
  226.2 45.4 %collective-permute-start.9 = (bf16[128,1152]{1,0:T(8,128)(2,1)S(1)}, bf16[128,1152]{1,0:T(8,128)(2,1)S(1)}, u32[]{:S(2)}, u32[]{:S(2)}) collective-permute-start(bf16[128,1152]{1,0:T(8,128)(2,1)S(1)} %convolution_convert_fusion.3), channel_id=1, source_target_pairs={{0,0},{896,1},{544,2},{416,3},{256,4},{128,5},{800,6},{672,7},{512... | collective-permute-start | bytes 884744 | tf_op jit(solution)/shard_map/ppermute | solution.py:55
  271.6 0.0 collective-permute-done.10
  271.6 16.0 %collective-permute-done.9 = bf16[128,1152]{1,0:T(8,128)(2,1)S(1)} collective-permute-done((bf16[128,1152]{1,0:T(8,128)(2,1)S(1)}, bf16[128,1152]{1,0:T(8,128)(2,1)S(1)}, u32[]{:S(2)}, u32[]{:S(2)}) %collective-permute-start.9) | collective-permute-done | bytes 294944 | tf_op jit(solution)/shard_map/ppermute | solution.py:55
  287.6 0.7 copy.11
  288.3 0.7 copy.12
  (1 shorter events, 0.0 us)
Async XLA Ops:
  0.6 29.2 %collective-permute-start = (bf16[128,1152]{1,0:T(8,128)(2,1)}, bf16[128,1152]{1,0:T(8,128)(2,1)S(1)}, u32[]{:S(2)}, u32[]{:S(2)}) collective-permute-start(bf16[128,1152]{1,0:T(8,128)(2,1)} %param.6), channel_id=1, source_target_pairs={{0,0},{1,897},{2,546},{3,419},{4,260},{5,133},{6,806},{7,679},{8,5... | collective-permute-start | bytes 884744 | tf_op jit(solution)/shard_map/ppermute | solution.py:55
  7.4 22.4 %collective-permute-start.1 = (s32[128]{0:T(128)}, s32[128]{0:T(128)S(1)}, u32[]{:S(2)}, u32[]{:S(2)}) collective-permute-start(s32[128]{0:T(128)} %param.7), channel_id=1, source_target_pairs={{0,0},{1,896},{2,544},{3,416},{4,256},{5,128},{6,800},{7,672},{8,5... | collective-permute-start | bytes 1544 | tf_op jit(solution)/shard_map/ppermute | solution.py:55
  29.8 16.3 %collective-permute-start.2 = (bf16[128,1152]{1,0:T(8,128)(2,1)}, bf16[128,1152]{1,0:T(8,128)(2,1)S(1)}, u32[]{:S(2)}, u32[]{:S(2)}) collective-permute-start(bf16[128,1152]{1,0:T(8,128)(2,1)} %param.5), channel_id=1, source_target_pairs={{0,0},{1,897},{2,546},{3,419},{4,260},{5,133},{6,806},{7,679},{8,5... | collective-permute-start | bytes 884744 | tf_op jit(solution)/shard_map/ppermute | solution.py:55
  35.5 35.1 %collective-permute-start.4 = (bf16[128,1152]{1,0:T(8,128)(2,1)S(1)}, bf16[128,1152]{1,0:T(8,128)(2,1)S(1)}, u32[]{:S(2)}, u32[]{:S(2)}) collective-permute-start(bf16[128,1152]{1,0:T(8,128)(2,1)S(1)} %collective-permute-done), channel_id=1, source_target_pairs={{0,0},{897,896},{546,544},{419,416},{260,256},{133,128},{806,800},... | collective-permute-start | bytes 884744 | tf_op jit(solution)/shard_map/ppermute | solution.py:55
  46.2 43.3 %collective-permute-start.3 = (bf16[128,1152]{1,0:T(8,128)(2,1)S(1)}, bf16[128,1152]{1,0:T(8,128)(2,1)S(1)}, u32[]{:S(2)}, u32[]{:S(2)}) collective-permute-start(bf16[128,1152]{1,0:T(8,128)(2,1)S(1)} %collective-permute-done.2), channel_id=1, source_target_pairs={{0,0},{897,896},{546,544},{419,416},{260,256},{133,128},{806,800},... | collective-permute-start | bytes 884744 | tf_op jit(solution)/shard_map/ppermute | solution.py:55
  136.0 9.6 %collective-permute-start.5 = (bf16[256,1152]{1,0:T(8,128)(2,1)S(1)}, bf16[256,1152]{1,0:T(8,128)(2,1)}, u32[]{:S(2)}, u32[]{:S(2)}) collective-permute-start(bf16[256,1152]{1,0:T(8,128)(2,1)S(1)} %get-tuple-element.15), channel_id=1, source_target_pairs={{0,64},{64,128},{128,192},{192,32},{32,96},{96,160},{160,224},{224... | collective-permute-start | bytes 1769480 | tf_op jit(solution)/shard_map/ppermute | solution.py:55
  140.1 11.3 %collective-permute-start.7 = (bf16[256,1152]{1,0:T(8,128)(2,1)S(1)}, bf16[256,1152]{1,0:T(8,128)(2,1)}, u32[]{:S(2)}, u32[]{:S(2)}) collective-permute-start(bf16[256,1152]{1,0:T(8,128)(2,1)S(1)} %get-tuple-element.14), channel_id=1, source_target_pairs={{64,0},{128,64},{192,128},{32,192},{96,32},{160,96},{224,160},{416... | collective-permute-start | bytes 1769480 | tf_op jit(solution)/shard_map/ppermute | solution.py:55
  145.6 11.6 %collective-permute-start.6 = (bf16[256,1152]{1,0:T(8,128)(2,1)}, bf16[256,1152]{1,0:T(8,128)(2,1)}, u32[]{:S(2)}, u32[]{:S(2)}) collective-permute-start(bf16[256,1152]{1,0:T(8,128)(2,1)} %collective-permute-done.5), channel_id=1, source_target_pairs={{0,64},{64,128},{128,192},{192,32},{32,96},{96,160},{160,224},{224... | collective-permute-start | bytes 1769480 | tf_op jit(solution)/shard_map/ppermute | solution.py:55
  151.4 11.5 %collective-permute-start.8 = (bf16[256,1152]{1,0:T(8,128)(2,1)}, bf16[256,1152]{1,0:T(8,128)(2,1)}, u32[]{:S(2)}, u32[]{:S(2)}) collective-permute-start(bf16[256,1152]{1,0:T(8,128)(2,1)} %collective-permute-done.7), channel_id=1, source_target_pairs={{64,0},{128,64},{192,128},{32,192},{96,32},{160,96},{224,160},{416... | collective-permute-start | bytes 1769480 | tf_op jit(solution)/shard_map/ppermute | solution.py:55
  167.5 22.1 %copy-start = (bf16[256,1152]{1,0:T(8,128)(2,1)S(1)}, bf16[256,1152]{1,0:T(8,128)(2,1)}, u32[]{:S(2)}) copy-start(bf16[256,1152]{1,0:T(8,128)(2,1)} %fusion) | copy-start | bytes 1769476
  168.5 31.9 %all-to-all-start.2 = ((bf16[64,4,1152]{2,1,0:T(4,128)(2,1)}), bf16[64,4,1152]{2,1,0:T(4,128)(2,1)S(1)}, u32[]{:S(2)}, u32[]{:S(2)}) async-start(bf16[64,4,1152]{2,1,0:T(4,128)(2,1)} %reshape.30), calls=%async_computation.2 | async-start | bytes 1179648 | tf_op jit(solution)/shard_map/all_to_all | solution.py:81
  200.3 25.4 %all-to-all-start.1 = ((bf16[64,4,1152]{2,1,0:T(4,128)(2,1)}), bf16[64,4,1152]{2,1,0:T(4,128)(2,1)S(1)}, u32[]{:S(2)}, u32[]{:S(2)}) async-start(bf16[64,4,1152]{2,1,0:T(4,128)(2,1)} %reshape.28), calls=%async_computation.1 | async-start | bytes 1179648 | tf_op jit(solution)/shard_map/all_to_all | solution.py:81
  207.6 64.0 %collective-permute-start.10 = (bf16[128,1152]{1,0:T(8,128)(2,1)S(1)}, bf16[128,1152]{1,0:T(8,128)(2,1)S(1)}, u32[]{:S(2)}, u32[]{:S(2)}) collective-permute-start(bf16[128,1152]{1,0:T(8,128)(2,1)S(1)} %convolution_convert_fusion.2), channel_id=1, source_target_pairs={{0,0},{896,1},{544,2},{416,3},{256,4},{128,5},{800,6},{672,7},{512... | collective-permute-start | bytes 884744 | tf_op jit(solution)/shard_map/ppermute | solution.py:55
  226.2 61.4 %collective-permute-start.9 = (bf16[128,1152]{1,0:T(8,128)(2,1)S(1)}, bf16[128,1152]{1,0:T(8,128)(2,1)S(1)}, u32[]{:S(2)}, u32[]{:S(2)}) collective-permute-start(bf16[128,1152]{1,0:T(8,128)(2,1)S(1)} %convolution_convert_fusion.3), channel_id=1, source_target_pairs={{0,0},{896,1},{544,2},{416,3},{256,4},{128,5},{800,6},{672,7},{512... | collective-permute-start | bytes 884744 | tf_op jit(solution)/shard_map/ppermute | solution.py:55

commit v4 on v2

--- a/solution.py
+++ b/solution.py
@@ -18,10 +18,11 @@
     for g in range(GRP):
         for y_hi in range(Y_HI):
             for z in range(Z):
-                column = (g - z + 8 * y_hi) % GRP
+                column = (3 * g + z + 8 * y_hi) % GRP
+                z_lo = (2 * g - z) % Z // GRP
                 source = (g * Y_HI + y_hi) * Z + z
                 via = device_at(column // 4, column % 4, y_hi, z)
-                held = device_at(column // 4, column % 4, y_hi, 2 * g + z // GRP)
+                held = device_at(column // 4, column % 4, y_hi, 2 * g + z_lo)
                 in_plane.append((source, via))
                 along_z.append((via, held))
     return in_plane, along_z
@@ -89,7 +90,7 @@
 
 
 def body(picture_embeds, caption_embeds, holder_position, score_scaling, score_offset_term):
-    rows_here = picture_embeds.shape[0]
+    rows_here, width = picture_embeds.shape
     devices = lax.axis_size(REGION)
     capacity = 2 * rows_here // devices
     slots = devices * capacity
@@ -97,10 +98,8 @@
     offset = score_offset_term[0]
 
     position = moved(holder_position, TO_REGION)
-    captions_via = moved(caption_embeds, IN_PLANE)
-    pictures_via = moved(picture_embeds, IN_PLANE)
-    captions_held = moved(captions_via, ALONG_Z)
-    pictures_held = moved(pictures_via, ALONG_Z)
+    both = jnp.concatenate([picture_embeds, caption_embeds], axis=1)
+    held = moved(moved(both, IN_PLANE), ALONG_Z)
 
     same = position[:, None] == position[None, :]
     order = jnp.arange(rows_here, dtype=jnp.int32)
@@ -111,8 +110,9 @@
         jnp.arange(slots, dtype=jnp.int32)[:, None] == (owner * capacity + rank_in)[None, :]
     ).astype(jnp.bfloat16)
 
-    captions = swap_blocks(times_rows(placer, captions_held).astype(jnp.bfloat16), devices)
-    pictures = swap_blocks(times_rows(placer, pictures_held).astype(jnp.bfloat16), devices)
+    received = swap_blocks(times_rows(placer, held).astype(jnp.bfloat16), devices)
+    pictures = received[:, :width]
+    captions = received[:, width:]
 
     earlier_captions = [captions]
     later_pictures = [pictures]
@@ -128,15 +128,13 @@
     for step in range(1, STEPS + 1):
         weights = weight_matrix(pictures, earlier_captions[step], scale, offset, zero)
         image_total = image_total + times_rows(weights, earlier_captions[step])
-    image_back = swap_blocks(image_total.astype(jnp.bfloat16), devices)
-    for step in range(1, STEPS + 1):
         weights = weight_matrix(later_pictures[step], captions, scale, offset, zero)
         text_total = text_total + rows_of_transpose(weights, later_pictures[step])
-    text_back = swap_blocks(text_total.astype(jnp.bfloat16), devices)
 
-    image_grad = moved(rows_of_transpose(placer, image_back).astype(jnp.bfloat16), FROM_REGION)
-    text_grad = moved(rows_of_transpose(placer, text_back).astype(jnp.bfloat16), FROM_REGION)
-    return (image_grad, text_grad)
+    done = jnp.concatenate([image_total, text_total], axis=1).astype(jnp.bfloat16)
+    back = swap_blocks(done, devices)
+    grads = moved(rows_of_transpose(placer, back).astype(jnp.bfloat16), FROM_REGION)
+    return (grads[:, :width], grads[:, width:])
 
 
 def solution(mesh):

time: 317 us -> 259 us (0.82)
  the two profiles are of different devices: /device:TPU:27 before, /device:TPU:21 now
where the time goes in v4:
time: 259 us; the launch traced here: 258 us
  waiting for transfers between devices  125 us (48%)
  starting transfers between devices  83.2 us (32%)
  blocking collectives  28.2 us (11%)
  matrix products  13.1 us (5%)
  local copies, waits for them, and re-layouts  4.39 us (2%)
    ppermute x8, waiting for transfers between devices, moved(): return lax.ppermute(x, AXES, route)  111 us
    ppermute x8, starting transfers between devices, moved(): return lax.ppermute(x, AXES, route)  61.5 us
    all_to_all x1, blocking collectives, swap_blocks(): lax.all_to_all(x.reshape(devices, slots // devices, width), REGION, split...  28.2 us
    all_to_all x1, starting transfers between devices, swap_blocks(): lax.all_to_all(x.reshape(devices, slots // devices, width), REGION, split...  21.7 us
    all_to_all x1, waiting for transfers between devices, swap_blocks(): lax.all_to_all(x.reshape(devices, slots // devices, width), REGION, split...  14 us
    dot_general x4, matrix products, times_rows(): return jnp.dot(weights, rows, preferred_element_type=jnp.float32)  6.57 us
    dot_general x4, matrix products, rows_of_transpose(): lax.dot_general(weights, rows, (((0,), (0,)), ((), ())), preferred_elemen...  6.11 us
  transfers between devices with their start and end apart: 9, of which 6 were waited for; matrix products, arithmetic and copies ran while one was open for 4% of the time, Pallas kernels for 0%

profile of v4, /device:TPU:21, one launch (start us, length us, event | category | flops | bytes accessed | tf_op | source)
XLA Modules:
  0.0 258.0 jit_solution(5349982900992595560)
XLA Ops:
  0.6 0.0 copy-start
  0.6 1.1 pad_maximum_fusion.1
  1.7 2.9 %collective-permute-start.1 = (bf16[128,2304]{1,0:T(8,128)(2,1)S(1)}, bf16[128,2304]{1,0:T(8,128)(2,1)S(1)}, u32[]{:S(2)}, u32[]{:S(2)}) collective-permute-start(bf16[128,2304]{1,0:T(8,128)(2,1)S(1)} %pad_maximum_fusion.1), channel_id=1, source_target_pairs={{0,0},{1,129},{2,34},{3,163},{4,260},{5,389},{6,294},{7,423},{8,52... | collective-permute-start | bytes 1769480 | tf_op jit(solution)/shard_map/ppermute | solution.py:56
  4.6 13.1 %collective-permute-done.1 = bf16[128,2304]{1,0:T(8,128)(2,1)S(1)} collective-permute-done((bf16[128,2304]{1,0:T(8,128)(2,1)S(1)}, bf16[128,2304]{1,0:T(8,128)(2,1)S(1)}, u32[]{:S(2)}, u32[]{:S(2)}) %collective-permute-start.1) | collective-permute-done | bytes 589856 | tf_op jit(solution)/shard_map/ppermute | solution.py:56
  17.7 22.4 %collective-permute-start.2 = (bf16[128,2304]{1,0:T(8,128)(2,1)S(1)}, bf16[128,2304]{1,0:T(8,128)(2,1)S(1)}, u32[]{:S(2)}, u32[]{:S(2)}) collective-permute-start(bf16[128,2304]{1,0:T(8,128)(2,1)S(1)} %collective-permute-done.1), channel_id=1, source_target_pairs={{0,0},{129,129},{34,33},{163,161},{260,257},{389,385},{294,289},{4... | collective-permute-start | bytes 1769480 | tf_op jit(solution)/shard_map/ppermute | solution.py:56
  40.1 0.0 copy-done
  40.1 5.5 %collective-permute-start = (s32[128]{0:T(128)S(1)}, s32[128]{0:T(128)S(1)}, u32[]{:S(2)}, u32[]{:S(2)}) collective-permute-start(s32[128]{0:T(128)S(1)} %copy-done), channel_id=1, source_target_pairs={{0,0},{1,129},{2,33},{3,161},{4,257},{5,385},{6,289},{7,417},{8,51... | collective-permute-start | bytes 1544 | tf_op jit(solution)/shard_map/ppermute | solution.py:56
  45.7 39.2 %collective-permute-done = s32[128]{0:T(128)S(1)} collective-permute-done((s32[128]{0:T(128)S(1)}, s32[128]{0:T(128)S(1)}, u32[]{:S(2)}, u32[]{:S(2)}) %collective-permute-start) | collective-permute-done | bytes 544 | tf_op jit(solution)/shard_map/ppermute | solution.py:56
  84.9 0.2 convert_reduce_fusion
  85.1 0.0 collective-permute-done.2
  85.1 0.5 convolution_convert_fusion
  85.5 1.2 reshape.21
  86.7 21.7 %all-to-all-start = ((bf16[64,4,2304]{2,1,0:T(4,128)(2,1)}), bf16[64,4,2304]{2,1,0:T(4,128)(2,1)S(1)}, u32[]{:S(2)}, u32[]{:S(2)}) async-start(bf16[64,4,2304]{2,1,0:T(4,128)(2,1)} %reshape.21), calls=%async_computation | async-start | bytes 2359296 | tf_op jit(solution)/shard_map/all_to_all | solution.py:82
  109.7 14.0 %all-to-all-done = bf16[64,4,2304]{2,1,0:T(4,128)(2,1)S(1)} async-done(((bf16[64,4,2304]{2,1,0:T(4,128)(2,1)}), bf16[64,4,2304]{2,1,0:T(4,128)(2,1)S(1)}, u32[]{:S(2)}, u32[]{:S(2)}) %all-to-all-start) | async-done | bytes 1179680 | tf_op jit(solution)/shard_map/all_to_all | solution.py:82
  123.7 0.3 reshape.22
  124.0 0.1 fusion.72
  124.1 3.4 %collective-permute-start.3 = (bf16[256,1152]{1,0:T(8,128)(2,1)S(1)}, bf16[256,1152]{1,0:T(8,128)(2,1)}, u32[]{:S(2)}, u32[]{:S(2)}) collective-permute-start(bf16[256,1152]{1,0:T(8,128)(2,1)S(1)} %get-tuple-element.2), channel_id=1, source_target_pairs={{0,64},{64,128},{128,192},{192,32},{32,96},{96,160},{160,224},{224... | collective-permute-start | bytes 1769480 | tf_op jit(solution)/shard_map/ppermute | solution.py:56
  127.5 1.9 collective-permute-start.5
  129.4 0.4 fusion.33
  129.8 0.3 fusion.62
  130.2 0.4 fusion.65
  130.5 3.8 %collective-permute-done.3 = bf16[256,1152]{1,0:T(8,128)(2,1)} collective-permute-done((bf16[256,1152]{1,0:T(8,128)(2,1)S(1)}, bf16[256,1152]{1,0:T(8,128)(2,1)}, u32[]{:S(2)}, u32[]{:S(2)}) %collective-permute-start.3) | collective-permute-done | bytes 589856 | tf_op jit(solution)/shard_map/ppermute | solution.py:56
  134.3 4.5 %collective-permute-start.4 = (bf16[256,1152]{1,0:T(8,128)(2,1)}, bf16[256,1152]{1,0:T(8,128)(2,1)}, u32[]{:S(2)}, u32[]{:S(2)}) collective-permute-start(bf16[256,1152]{1,0:T(8,128)(2,1)} %collective-permute-done.3), channel_id=1, source_target_pairs={{0,64},{64,128},{128,192},{192,32},{32,96},{96,160},{160,224},{224... | collective-permute-start | bytes 1769480 | tf_op jit(solution)/shard_map/ppermute | solution.py:56
  138.8 0.0 collective-permute-done.5
  138.8 1.9 collective-permute-start.6
  140.7 3.2 %convolution_add_fusion.3 = f32[256,1152]{1,0:T(8,128)} fusion(f32[256,1152]{1,0:T(8,128)S(1)} %fusion.62, bf16[256,1152]{1,0:T(8,128)(2,1)} %collective-permute-done.3, f32[]{:T(128)} %bitcast.23, f32[]{:T(128)} %bitcast.16, bf16[256,2304]{1,0:T(8,128)(2,1)S(1)} %reshape.22), kind=kOutput, calls=%fused_computation.5 | convolution fusion | flops 302743552 | bytes 4129792 | tf_op jit(solution)/shard_map/dot_general | solution.py:71
  143.9 2.3 convolution_add_fusion.1
  146.2 0.0 collective-permute-done.4
  146.2 2.6 fusion
  148.8 0.1 concatenate.13
  149.0 1.4 collective-permute-done.6
  150.3 3.1 %fusion.1 = bf16[256,1152]{1,0:T(8,128)(2,1)} fusion(f32[256,1152]{1,0:T(8,128)S(1)} %convolution_add_fusion.1, bf16[256,1152]{1,0:T(8,128)(2,1)} %collective-permute-done.6, f32[]{:T(128)} %bitcast.20, f32[]{:T(128)} %bitcast.17, bf16[256,2304]{1,0:T(8,128)(2,1)S(1)} %reshape.22), kind=kOutput, calls=%fused_computation.7 | convolution fusion | flops 303038464 | bytes 3539968 | tf_op jit(solution)/shard_map/dot_general | solution.py:75
  153.4 1.5 concatenate.14
  155.0 0.5 pad_maximum_fusion
  155.5 28.2 %all_to_all.10 = bf16[64,4,2304]{2,1,0:T(4,128)(2,1)S(1)} all-to-all(bf16[64,4,2304]{2,1,0:T(4,128)(2,1)S(1)} %pad_maximum_fusion), channel_id=1, replica_groups=mesh['grp'=16,'y_hi'=2,'z_hi'=16,'z_lo'=2] {'grp','y_hi','z_lo'}, dimensions={0} | all-to-all | bytes 2359296 | tf_op jit(solution)/shard_map/all_to_all | solution.py:82
  183.7 0.3 reshape.23
  184.0 0.4 convolution_convert_fusion.1
  184.4 19.0 %collective-permute-start.7 = (bf16[128,2304]{1,0:T(8,128)(2,1)S(1)}, bf16[128,2304]{1,0:T(8,128)(2,1)S(1)}, u32[]{:S(2)}, u32[]{:S(2)}) collective-permute-start(bf16[128,2304]{1,0:T(8,128)(2,1)S(1)} %convolution_convert_fusion.1), channel_id=1, source_target_pairs={{0,0},{129,1},{33,2},{161,3},{257,4},{385,5},{289,6},{417,7},{513,... | collective-permute-start | bytes 1769480 | tf_op jit(solution)/shard_map/ppermute | solution.py:56
  203.4 53.7 %collective-permute-done.7 = bf16[128,2304]{1,0:T(8,128)(2,1)S(1)} collective-permute-done((bf16[128,2304]{1,0:T(8,128)(2,1)S(1)}, bf16[128,2304]{1,0:T(8,128)(2,1)S(1)}, u32[]{:S(2)}, u32[]{:S(2)}) %collective-permute-start.7) | collective-permute-done | bytes 589856 | tf_op jit(solution)/shard_map/ppermute | solution.py:56
  257.1 0.9 fusion.73
  (1 shorter events, 0.0 us)
Async XLA Ops:
  0.6 39.5 %copy-start = (s32[128]{0:T(128)S(1)}, s32[128]{0:T(128)}, u32[]{:S(2)}) copy-start(s32[128]{0:T(128)} %param.7) | copy-start | bytes 1540
  1.7 16.0 %collective-permute-start.1 = (bf16[128,2304]{1,0:T(8,128)(2,1)S(1)}, bf16[128,2304]{1,0:T(8,128)(2,1)S(1)}, u32[]{:S(2)}, u32[]{:S(2)}) collective-permute-start(bf16[128,2304]{1,0:T(8,128)(2,1)S(1)} %pad_maximum_fusion.1), channel_id=1, source_target_pairs={{0,0},{1,129},{2,34},{3,163},{4,260},{5,389},{6,294},{7,423},{8,52... | collective-permute-start | bytes 1769480 | tf_op jit(solution)/shard_map/ppermute | solution.py:56
  17.7 67.3 %collective-permute-start.2 = (bf16[128,2304]{1,0:T(8,128)(2,1)S(1)}, bf16[128,2304]{1,0:T(8,128)(2,1)S(1)}, u32[]{:S(2)}, u32[]{:S(2)}) collective-permute-start(bf16[128,2304]{1,0:T(8,128)(2,1)S(1)} %collective-permute-done.1), channel_id=1, source_target_pairs={{0,0},{129,129},{34,33},{163,161},{260,257},{389,385},{294,289},{4... | collective-permute-start | bytes 1769480 | tf_op jit(solution)/shard_map/ppermute | solution.py:56
  40.1 44.7 %collective-permute-start = (s32[128]{0:T(128)S(1)}, s32[128]{0:T(128)S(1)}, u32[]{:S(2)}, u32[]{:S(2)}) collective-permute-start(s32[128]{0:T(128)S(1)} %copy-done), channel_id=1, source_target_pairs={{0,0},{1,129},{2,33},{3,161},{4,257},{5,385},{6,289},{7,417},{8,51... | collective-permute-start | bytes 1544 | tf_op jit(solution)/shard_map/ppermute | solution.py:56
  86.7 36.9 %all-to-all-start = ((bf16[64,4,2304]{2,1,0:T(4,128)(2,1)}), bf16[64,4,2304]{2,1,0:T(4,128)(2,1)S(1)}, u32[]{:S(2)}, u32[]{:S(2)}) async-start(bf16[64,4,2304]{2,1,0:T(4,128)(2,1)} %reshape.21), calls=%async_computation | async-start | bytes 2359296 | tf_op jit(solution)/shard_map/all_to_all | solution.py:82
  124.1 10.2 %collective-permute-start.3 = (bf16[256,1152]{1,0:T(8,128)(2,1)S(1)}, bf16[256,1152]{1,0:T(8,128)(2,1)}, u32[]{:S(2)}, u32[]{:S(2)}) collective-permute-start(bf16[256,1152]{1,0:T(8,128)(2,1)S(1)} %get-tuple-element.2), channel_id=1, source_target_pairs={{0,64},{64,128},{128,192},{192,32},{32,96},{96,160},{160,224},{224... | collective-permute-start | bytes 1769480 | tf_op jit(solution)/shard_map/ppermute | solution.py:56
  127.5 11.3 %collective-permute-start.5 = (bf16[256,1152]{1,0:T(8,128)(2,1)S(1)}, bf16[256,1152]{1,0:T(8,128)(2,1)}, u32[]{:S(2)}, u32[]{:S(2)}) collective-permute-start(bf16[256,1152]{1,0:T(8,128)(2,1)S(1)} %get-tuple-element.3), channel_id=1, source_target_pairs={{64,0},{128,64},{192,128},{32,192},{96,32},{160,96},{224,160},{416... | collective-permute-start | bytes 1769480 | tf_op jit(solution)/shard_map/ppermute | solution.py:56
  134.3 11.9 %collective-permute-start.4 = (bf16[256,1152]{1,0:T(8,128)(2,1)}, bf16[256,1152]{1,0:T(8,128)(2,1)}, u32[]{:S(2)}, u32[]{:S(2)}) collective-permute-start(bf16[256,1152]{1,0:T(8,128)(2,1)} %collective-permute-done.3), channel_id=1, source_target_pairs={{0,64},{64,128},{128,192},{192,32},{32,96},{96,160},{160,224},{224... | collective-permute-start | bytes 1769480 | tf_op jit(solution)/shard_map/ppermute | solution.py:56
  138.8 11.5 %collective-permute-start.6 = (bf16[256,1152]{1,0:T(8,128)(2,1)}, bf16[256,1152]{1,0:T(8,128)(2,1)}, u32[]{:S(2)}, u32[]{:S(2)}) collective-permute-start(bf16[256,1152]{1,0:T(8,128)(2,1)} %collective-permute-done.5), channel_id=1, source_target_pairs={{64,0},{128,64},{192,128},{32,192},{96,32},{160,96},{224,160},{416... | collective-permute-start | bytes 1769480 | tf_op jit(solution)/shard_map/ppermute | solution.py:56
  184.4 72.8 %collective-permute-start.7 = (bf16[128,2304]{1,0:T(8,128)(2,1)S(1)}, bf16[128,2304]{1,0:T(8,128)(2,1)S(1)}, u32[]{:S(2)}, u32[]{:S(2)}) collective-permute-start(bf16[128,2304]{1,0:T(8,128)(2,1)S(1)} %convolution_convert_fusion.1), channel_id=1, source_target_pairs={{0,0},{129,1},{33,2},{161,3},{257,4},{385,5},{289,6},{417,7},{513,... | collective-permute-start | bytes 1769480 | tf_op jit(solution)/shard_map/ppermute | solution.py:56

commit v5 on v4

--- a/solution.py
+++ b/solution.py
@@ -1,6 +1,8 @@
 import jax
 import jax.numpy as jnp
 from jax import lax
+from jax.experimental import pallas as pl
+from jax.experimental.pallas import tpu as pltpu
 from jax.sharding import Mesh, PartitionSpec as P
 
 STEPS = 2
@@ -56,15 +58,53 @@
     return lax.ppermute(x, AXES, route)
 
 
-def weight_matrix(picture_batch, caption_batch, scale, offset, matching_label):
-    scores = lax.dot_general(
-        picture_batch,
-        caption_batch,
-        (((1,), (1,)), ((), ())),
-        preferred_element_type=jnp.float32,
-    )
-    pair_scores = scale * scores + offset
-    return (scale * (jax.nn.sigmoid(pair_scores) - matching_label)).astype(jnp.bfloat16)
+TILE = 384
+
+
+def gradients_kernel(scale_ref, offset_ref, p0, p1, p2, c0, c1, c2, out_ref):
+    slots, width = p0.shape
+    scale, offset = scale_ref[0], offset_ref[0]
+    shape = (slots, slots)
+    same = lax.broadcasted_iota(jnp.int32, shape, 0) == lax.broadcasted_iota(jnp.int32, shape, 1)
+    identity_square = jnp.where(same, jnp.float32(1.0), jnp.float32(0.0))
+
+    def weights(left, right, matching_label):
+        scores = lax.dot_general(
+            left[...], right[...], (((1,), (1,)), ((), ())), preferred_element_type=jnp.float32
+        )
+        coef = jax.nn.sigmoid(scale * scores + offset) - matching_label
+        return (scale * coef).astype(jnp.bfloat16)
+
+    zero = jnp.float32(0.0)
+    for rows, others, start in ((p0, (c0, c1, c2), 0), (c0, (p0, p1, p2), width)):
+        mixed = [
+            weights(rows, other, identity_square if n == 0 else zero)
+            for n, other in enumerate(others)
+        ]
+        for at in range(0, width, TILE):
+            total = sum(
+                jnp.dot(w, other[:, at : at + TILE], preferred_element_type=jnp.float32)
+                for w, other in zip(mixed, others)
+            )
+            out_ref[:, start + at : start + at + TILE] = total.astype(out_ref.dtype)
+
+
+def gradients(scale, offset, pictures, captions):
+    slots, width = pictures[0].shape
+    arrays = [*pictures, *captions]
+    flops = 12 * 2 * slots * slots * width
+    return pl.pallas_call(
+        gradients_kernel,
+        out_shape=jax.ShapeDtypeStruct((slots, 2 * width), jnp.bfloat16),
+        in_specs=[pl.BlockSpec(memory_space=pltpu.SMEM)] * 2
+        + [pl.BlockSpec(memory_space=pltpu.VMEM)] * len(arrays),
+        out_specs=pl.BlockSpec(memory_space=pltpu.VMEM),
+        compiler_params=pltpu.CompilerParams(vmem_limit_bytes=24 * 1024 * 1024),
+        cost_estimate=pl.CostEstimate(
+            flops=flops, bytes_accessed=16 * slots * width, transcendentals=6 * slots * slots
+        ),
+        name="gradients",
+    )(scale, offset, *arrays)
 
 
 def times_rows(weights, rows):
@@ -94,8 +134,6 @@
     devices = lax.axis_size(REGION)
     capacity = 2 * rows_here // devices
     slots = devices * capacity
-    scale = score_scaling[0]
-    offset = score_offset_term[0]
 
     position = moved(holder_position, TO_REGION)
     both = jnp.concatenate([picture_embeds, caption_embeds], axis=1)
@@ -120,18 +158,7 @@
         earlier_captions.append(moved(earlier_captions[-1], NEXT))
         later_pictures.append(moved(later_pictures[-1], BEFORE))
 
-    identity_square = jnp.eye(slots, dtype=jnp.float32)
-    own_weights = weight_matrix(pictures, captions, scale, offset, identity_square)
-    image_total = times_rows(own_weights, captions)
-    text_total = rows_of_transpose(own_weights, pictures)
-    zero = jnp.float32(0.0)
-    for step in range(1, STEPS + 1):
-        weights = weight_matrix(pictures, earlier_captions[step], scale, offset, zero)
-        image_total = image_total + times_rows(weights, earlier_captions[step])
-        weights = weight_matrix(later_pictures[step], captions, scale, offset, zero)
-        text_total = text_total + rows_of_transpose(weights, later_pictures[step])
-
-    done = jnp.concatenate([image_total, text_total], axis=1).astype(jnp.bfloat16)
+    done = gradients(score_scaling, score_offset_term, later_pictures, earlier_captions)
     back = swap_blocks(done, devices)
     grads = moved(rows_of_transpose(placer, back).astype(jnp.bfloat16), FROM_REGION)
     return (grads[:, :width], grads[:, width:])

time: 259 us -> 254 us (0.981)
  the two profiles are of different devices: /device:TPU:21 before, /device:TPU:20 now
where the time goes in v5:
time: 254 us; the launch traced here: 253 us
  waiting for transfers between devices  98.8 us (39%)
  blocking collectives  76.9 us (30%)
  starting transfers between devices  68.5 us (27%)
  Pallas kernels  2.69 us (1%)
    ppermute x8, waiting for transfers between devices, moved(): return lax.ppermute(x, AXES, route)  98.8 us
    all_to_all x2, blocking collectives, swap_blocks(): lax.all_to_all(x.reshape(devices, slots // devices, width), REGION, split...  76.9 us
    ppermute x8, starting transfers between devices, moved(): return lax.ppermute(x, AXES, route)  68.5 us
  transfers between devices with their start and end apart: 8, of which 7 were waited for; matrix products, arithmetic and copies ran while one was open for 0% of the time, Pallas kernels for 0%

profile of v5, /device:TPU:20, one launch (start us, length us, event | category | flops | bytes accessed | tf_op | source)
XLA Modules:
  0.0 253.3 jit_solution(6181179049820550128)
XLA Ops:
  0.6 0.0 copy-start
  0.6 1.1 pad_maximum_fusion
  1.7 1.9 collective-permute-start.1
  3.7 13.6 %collective-permute-done.1 = bf16[128,2304]{1,0:T(8,128)(2,1)S(1)} collective-permute-done((bf16[128,2304]{1,0:T(8,128)(2,1)S(1)}, bf16[128,2304]{1,0:T(8,128)(2,1)S(1)}, u32[]{:S(2)}, u32[]{:S(2)}) %collective-permute-start.1) | collective-permute-done | bytes 589856 | tf_op jit(solution)/shard_map/ppermute | solution.py:58
  17.3 20.5 %collective-permute-start.2 = (bf16[128,2304]{1,0:T(8,128)(2,1)S(1)}, bf16[128,2304]{1,0:T(8,128)(2,1)S(1)}, u32[]{:S(2)}, u32[]{:S(2)}) collective-permute-start(bf16[128,2304]{1,0:T(8,128)(2,1)S(1)} %collective-permute-done.1), channel_id=1, source_target_pairs={{0,0},{129,129},{34,33},{163,161},{260,257},{389,385},{294,289},{4... | collective-permute-start | bytes 1769480 | tf_op jit(solution)/shard_map/ppermute | solution.py:58
  37.8 0.0 copy-done
  37.8 18.8 %collective-permute-start = (s32[128]{0:T(128)S(1)}, s32[128]{0:T(128)S(1)}, u32[]{:S(2)}, u32[]{:S(2)}) collective-permute-start(s32[128]{0:T(128)S(1)} %copy-done), channel_id=1, source_target_pairs={{0,0},{1,129},{2,33},{3,161},{4,257},{5,385},{6,289},{7,417},{8,51... | collective-permute-start | bytes 1544 | tf_op jit(solution)/shard_map/ppermute | solution.py:58
  56.6 4.4 %collective-permute-done = s32[128]{0:T(128)S(1)} collective-permute-done((s32[128]{0:T(128)S(1)}, s32[128]{0:T(128)S(1)}, u32[]{:S(2)}, u32[]{:S(2)}) %collective-permute-start) | collective-permute-done | bytes 544 | tf_op jit(solution)/shard_map/ppermute | solution.py:58
  61.0 0.2 convert_reduce_fusion
  61.2 12.3 %collective-permute-done.2 = bf16[128,2304]{1,0:T(8,128)(2,1)S(1)} collective-permute-done((bf16[128,2304]{1,0:T(8,128)(2,1)S(1)}, bf16[128,2304]{1,0:T(8,128)(2,1)S(1)}, u32[]{:S(2)}, u32[]{:S(2)}) %collective-permute-start.2) | collective-permute-done | bytes 589856 | tf_op jit(solution)/shard_map/ppermute | solution.py:58
  73.5 0.5 convolution_convert_fusion
  74.0 0.3 reshape.19
  74.3 47.7 %all_to_all.10 = bf16[64,4,2304]{2,1,0:T(4,128)(2,1)S(1)} all-to-all(bf16[64,4,2304]{2,1,0:T(4,128)(2,1)S(1)} %reshape.19), channel_id=1, replica_groups=mesh['grp'=16,'y_hi'=2,'z_hi'=16,'z_lo'=2] {'grp','y_hi','z_lo'}, dimensions={0} | all-to-all | bytes 2359296 | tf_op jit(solution)/shard_map/all_to_all | solution.py:122
  122.0 0.3 reshape.20
  122.3 0.1 fusion.4
  122.4 2.3 collective-permute-start.5
  124.8 3.2 %collective-permute-start.3 = (bf16[256,1152]{1,0:T(8,128)(2,1)S(1)}, bf16[256,1152]{1,0:T(8,128)(2,1)S(1)}, u32[]{:S(2)}, u32[]{:S(2)}) collective-permute-start(bf16[256,1152]{1,0:T(8,128)(2,1)S(1)} %get-tuple-element.3.p0), channel_id=1, source_target_pairs={{64,0},{128,64},{192,128},{32,192},{96,32},{160,96},{224,160},{416... | collective-permute-start | bytes 1769480 | tf_op jit(solution)/shard_map/ppermute | solution.py:58
  128.0 5.6 %collective-permute-done.5.c1 = bf16[256,1152]{1,0:T(8,128)(2,1)S(1)} collective-permute-done((bf16[256,1152]{1,0:T(8,128)(2,1)S(1)}, bf16[256,1152]{1,0:T(8,128)(2,1)S(1)}, u32[]{:S(2)}, u32[]{:S(2)}) %collective-permute-start.5) | collective-permute-done | bytes 589856 | tf_op jit(solution)/shard_map/ppermute | solution.py:58
  133.6 1.9 collective-permute-start.6
  135.5 0.0 collective-permute-done.3.p1
  135.5 3.6 %collective-permute-start.4 = (bf16[256,1152]{1,0:T(8,128)(2,1)S(1)}, bf16[256,1152]{1,0:T(8,128)(2,1)S(1)}, u32[]{:S(2)}, u32[]{:S(2)}) collective-permute-start(bf16[256,1152]{1,0:T(8,128)(2,1)S(1)} %collective-permute-done.3.p1), channel_id=1, source_target_pairs={{64,0},{128,64},{192,128},{32,192},{96,32},{160,96},{224,160},{416... | collective-permute-start | bytes 1769480 | tf_op jit(solution)/shard_map/ppermute | solution.py:58
  140.5 4.3 %collective-permute-done.6.c2 = bf16[256,1152]{1,0:T(8,128)(2,1)S(1)} collective-permute-done((bf16[256,1152]{1,0:T(8,128)(2,1)S(1)}, bf16[256,1152]{1,0:T(8,128)(2,1)S(1)}, u32[]{:S(2)}, u32[]{:S(2)}) %collective-permute-start.6) | collective-permute-done | bytes 589856 | tf_op jit(solution)/shard_map/ppermute | solution.py:58
  144.8 1.8 collective-permute-done.4.p2
  146.6 2.7 %gradients.1 = bf16[256,2304]{1,0:T(8,128)(2,1)S(1)} custom-call(f32[1]{0:T(128)S(6)} %copy.7.scale_ref, f32[1]{0:T(128)S(6)} %copy.8.offset_ref, bf16[256,1152]{1,0:T(8,128)(2,1)S(1)} %get-tuple-element.3.p0, bf16[256,1152]{1,0:T(8,128)(2,1)S(1)} %collective-permute-done.3.p1, bf16[256,1152]{1,0:T(8,128)(2,1)S(1)} %collective-permute-done.4.p2, ...), custom_call_target="tpu_custom_call" | custom-call | flops 1811939328 | bytes 4718592 | tf_op jit(solution)/shard_map/gradients/pallas_call | solution.py:96
  149.3 0.3 reshape.21
  149.6 29.2 %all_to_all.11 = bf16[64,4,2304]{2,1,0:T(4,128)(2,1)S(1)} all-to-all(bf16[64,4,2304]{2,1,0:T(4,128)(2,1)S(1)} %reshape.21), channel_id=1, replica_groups=mesh['grp'=16,'y_hi'=2,'z_hi'=16,'z_lo'=2] {'grp','y_hi','z_lo'}, dimensions={0} | all-to-all | bytes 2359296 | tf_op jit(solution)/shard_map/all_to_all | solution.py:122
  178.8 0.3 reshape.22
  179.1 0.4 convolution_convert_fusion.1
  179.4 16.2 %collective-permute-start.7 = (bf16[128,2304]{1,0:T(8,128)(2,1)S(1)}, bf16[128,2304]{1,0:T(8,128)(2,1)S(1)}, u32[]{:S(2)}, u32[]{:S(2)}) collective-permute-start(bf16[128,2304]{1,0:T(8,128)(2,1)S(1)} %convolution_convert_fusion.1), channel_id=1, source_target_pairs={{0,0},{129,1},{33,2},{161,3},{257,4},{385,5},{289,6},{417,7},{513,... | collective-permute-start | bytes 1769480 | tf_op jit(solution)/shard_map/ppermute | solution.py:58
  195.6 56.8 %collective-permute-done.7 = bf16[128,2304]{1,0:T(8,128)(2,1)S(1)} collective-permute-done((bf16[128,2304]{1,0:T(8,128)(2,1)S(1)}, bf16[128,2304]{1,0:T(8,128)(2,1)S(1)}, u32[]{:S(2)}, u32[]{:S(2)}) %collective-permute-start.7) | collective-permute-done | bytes 589856 | tf_op jit(solution)/shard_map/ppermute | solution.py:58
  252.4 0.9 fusion.5
  (1 shorter events, 0.0 us)
Async XLA Ops:
  0.6 37.2 %copy-start = (s32[128]{0:T(128)S(1)}, s32[128]{0:T(128)}, u32[]{:S(2)}) copy-start(s32[128]{0:T(128)} %param.7) | copy-start | bytes 1540
  1.7 15.5 %collective-permute-start.1 = (bf16[128,2304]{1,0:T(8,128)(2,1)S(1)}, bf16[128,2304]{1,0:T(8,128)(2,1)S(1)}, u32[]{:S(2)}, u32[]{:S(2)}) collective-permute-start(bf16[128,2304]{1,0:T(8,128)(2,1)S(1)} %pad_maximum_fusion), channel_id=1, source_target_pairs={{0,0},{1,129},{2,34},{3,163},{4,260},{5,389},{6,294},{7,423},{8,52... | collective-permute-start | bytes 1769480 | tf_op jit(solution)/shard_map/ppermute | solution.py:58
  17.3 56.2 %collective-permute-start.2 = (bf16[128,2304]{1,0:T(8,128)(2,1)S(1)}, bf16[128,2304]{1,0:T(8,128)(2,1)S(1)}, u32[]{:S(2)}, u32[]{:S(2)}) collective-permute-start(bf16[128,2304]{1,0:T(8,128)(2,1)S(1)} %collective-permute-done.1), channel_id=1, source_target_pairs={{0,0},{129,129},{34,33},{163,161},{260,257},{389,385},{294,289},{4... | collective-permute-start | bytes 1769480 | tf_op jit(solution)/shard_map/ppermute | solution.py:58
  37.8 23.2 %collective-permute-start = (s32[128]{0:T(128)S(1)}, s32[128]{0:T(128)S(1)}, u32[]{:S(2)}, u32[]{:S(2)}) collective-permute-start(s32[128]{0:T(128)S(1)} %copy-done), channel_id=1, source_target_pairs={{0,0},{1,129},{2,33},{3,161},{4,257},{5,385},{6,289},{7,417},{8,51... | collective-permute-start | bytes 1544 | tf_op jit(solution)/shard_map/ppermute | solution.py:58
  122.4 11.2 %collective-permute-start.5 = (bf16[256,1152]{1,0:T(8,128)(2,1)S(1)}, bf16[256,1152]{1,0:T(8,128)(2,1)S(1)}, u32[]{:S(2)}, u32[]{:S(2)}) collective-permute-start(bf16[256,1152]{1,0:T(8,128)(2,1)S(1)} %get-tuple-element.2.c0), channel_id=1, source_target_pairs={{0,64},{64,128},{128,192},{192,32},{32,96},{96,160},{160,224},{224... | collective-permute-start | bytes 1769480 | tf_op jit(solution)/shard_map/ppermute | solution.py:58
  124.8 10.8 %collective-permute-start.3 = (bf16[256,1152]{1,0:T(8,128)(2,1)S(1)}, bf16[256,1152]{1,0:T(8,128)(2,1)S(1)}, u32[]{:S(2)}, u32[]{:S(2)}) collective-permute-start(bf16[256,1152]{1,0:T(8,128)(2,1)S(1)} %get-tuple-element.3.p0), channel_id=1, source_target_pairs={{64,0},{128,64},{192,128},{32,192},{96,32},{160,96},{224,160},{416... | collective-permute-start | bytes 1769480 | tf_op jit(solution)/shard_map/ppermute | solution.py:58
  133.6 11.2 %collective-permute-start.6 = (bf16[256,1152]{1,0:T(8,128)(2,1)S(1)}, bf16[256,1152]{1,0:T(8,128)(2,1)S(1)}, u32[]{:S(2)}, u32[]{:S(2)}) collective-permute-start(bf16[256,1152]{1,0:T(8,128)(2,1)S(1)} %collective-permute-done.5.c1), channel_id=1, source_target_pairs={{0,64},{64,128},{128,192},{192,32},{32,96},{96,160},{160,224},{224... | collective-permute-start | bytes 1769480 | tf_op jit(solution)/shard_map/ppermute | solution.py:58
  135.5 11.0 %collective-permute-start.4 = (bf16[256,1152]{1,0:T(8,128)(2,1)S(1)}, bf16[256,1152]{1,0:T(8,128)(2,1)S(1)}, u32[]{:S(2)}, u32[]{:S(2)}) collective-permute-start(bf16[256,1152]{1,0:T(8,128)(2,1)S(1)} %collective-permute-done.3.p1), channel_id=1, source_target_pairs={{64,0},{128,64},{192,128},{32,192},{96,32},{160,96},{224,160},{416... | collective-permute-start | bytes 1769480 | tf_op jit(solution)/shard_map/ppermute | solution.py:58
  179.4 73.0 %collective-permute-start.7 = (bf16[128,2304]{1,0:T(8,128)(2,1)S(1)}, bf16[128,2304]{1,0:T(8,128)(2,1)S(1)}, u32[]{:S(2)}, u32[]{:S(2)}) collective-permute-start(bf16[128,2304]{1,0:T(8,128)(2,1)S(1)} %convolution_convert_fusion.1), channel_id=1, source_target_pairs={{0,0},{129,1},{33,2},{161,3},{257,4},{385,5},{289,6},{417,7},{513,... | collective-permute-start | bytes 1769480 | tf_op jit(solution)/shard_map/ppermute | solution.py:58

commit v6 on v5

--- a/solution.py
+++ b/solution.py
@@ -137,7 +137,8 @@
 
     position = moved(holder_position, TO_REGION)
     both = jnp.concatenate([picture_embeds, caption_embeds], axis=1)
-    held = moved(moved(both, IN_PLANE), ALONG_Z)
+    via, position = lax.optimization_barrier((moved(both, IN_PLANE), position))
+    held = moved(via, ALONG_Z)
 
     same = position[:, None] == position[None, :]
     order = jnp.arange(rows_here, dtype=jnp.int32)

time: 254 us -> 254 us (level)
  the two profiles are of different devices: /device:TPU:20 before, /device:TPU:76 now
where the time goes in v6:
time: 254 us
  waiting for transfers between devices  118 us (46%)
  blocking collectives  74.3 us (29%)
  starting transfers between devices  52.9 us (21%)
  Pallas kernels  2.69 us (1%)
    ppermute x8, waiting for transfers between devices, moved(): return lax.ppermute(x, AXES, route)  118 us
    all_to_all x2, blocking collectives, swap_blocks(): lax.all_to_all(x.reshape(devices, slots // devices, width), REGION, split...  74.3 us
    ppermute x8, starting transfers between devices, moved(): return lax.ppermute(x, AXES, route)  52.9 us
  transfers between devices with their start and end apart: 8, of which 6 were waited for; matrix products, arithmetic and copies ran while one was open for 0% of the time, Pallas kernels for 0%

profile of v6, /device:TPU:76, one launch (start us, length us, event | category | flops | bytes accessed | tf_op | source)
XLA Modules:
  0.0 253.9 jit_solution(14466273802153245446)
XLA Ops:
  0.6 0.0 copy-start
  0.6 1.1 pad_maximum_fusion
  1.7 2.3 collective-permute-start
  4.1 0.0 copy-done
  4.1 26.6 %collective-permute-start.1 = (s32[128]{0:T(128)S(1)}, s32[128]{0:T(128)S(1)}, u32[]{:S(2)}, u32[]{:S(2)}) collective-permute-start(s32[128]{0:T(128)S(1)} %copy-done), channel_id=1, source_target_pairs={{0,0},{1,129},{2,33},{3,161},{4,257},{5,385},{6,289},{7,417},{8,51... | collective-permute-start | bytes 1544 | tf_op jit(solution)/shard_map/ppermute | solution.py:58
  30.6 2.0 collective-permute-done.1
  32.7 0.0 collective-permute-done
  32.7 5.0 %collective-permute-start.2 = (bf16[128,2304]{1,0:T(8,128)(2,1)S(1)}, bf16[128,2304]{1,0:T(8,128)(2,1)S(1)}, u32[]{:S(2)}, u32[]{:S(2)}) collective-permute-start(bf16[128,2304]{1,0:T(8,128)(2,1)S(1)} %collective-permute-done), channel_id=1, source_target_pairs={{0,0},{129,129},{34,33},{163,161},{260,257},{389,385},{294,289},{4... | collective-permute-start | bytes 1769480 | tf_op jit(solution)/shard_map/ppermute | solution.py:58
  37.7 0.2 convert_reduce_fusion
  37.9 44.7 %collective-permute-done.2 = bf16[128,2304]{1,0:T(8,128)(2,1)S(1)} collective-permute-done((bf16[128,2304]{1,0:T(8,128)(2,1)S(1)}, bf16[128,2304]{1,0:T(8,128)(2,1)S(1)}, u32[]{:S(2)}, u32[]{:S(2)}) %collective-permute-start.2) | collective-permute-done | bytes 589856 | tf_op jit(solution)/shard_map/ppermute | solution.py:58
  82.6 0.5 convolution_convert_fusion
  83.0 0.3 reshape.19
  83.3 42.4 %all_to_all.10 = bf16[64,4,2304]{2,1,0:T(4,128)(2,1)S(1)} all-to-all(bf16[64,4,2304]{2,1,0:T(4,128)(2,1)S(1)} %reshape.19), channel_id=1, replica_groups=mesh['grp'=16,'y_hi'=2,'z_hi'=16,'z_lo'=2] {'grp','y_hi','z_lo'}, dimensions={0} | all-to-all | bytes 2359296 | tf_op jit(solution)/shard_map/all_to_all | solution.py:122
  125.8 0.3 reshape.20
  126.1 0.1 fusion.4
  126.2 2.3 collective-permute-start.5
  128.4 3.3 %collective-permute-start.3 = (bf16[256,1152]{1,0:T(8,128)(2,1)S(1)}, bf16[256,1152]{1,0:T(8,128)(2,1)S(1)}, u32[]{:S(2)}, u32[]{:S(2)}) collective-permute-start(bf16[256,1152]{1,0:T(8,128)(2,1)S(1)} %get-tuple-element.7.p0), channel_id=1, source_target_pairs={{64,0},{128,64},{192,128},{32,192},{96,32},{160,96},{224,160},{416... | collective-permute-start | bytes 1769480 | tf_op jit(solution)/shard_map/ppermute | solution.py:58
  131.7 5.6 %collective-permute-done.5.c1 = bf16[256,1152]{1,0:T(8,128)(2,1)S(1)} collective-permute-done((bf16[256,1152]{1,0:T(8,128)(2,1)S(1)}, bf16[256,1152]{1,0:T(8,128)(2,1)S(1)}, u32[]{:S(2)}, u32[]{:S(2)}) %collective-permute-start.5) | collective-permute-done | bytes 589856 | tf_op jit(solution)/shard_map/ppermute | solution.py:58
  137.4 1.9 collective-permute-start.6
  139.3 0.0 collective-permute-done.3.p1
  139.3 3.6 %collective-permute-start.4 = (bf16[256,1152]{1,0:T(8,128)(2,1)S(1)}, bf16[256,1152]{1,0:T(8,128)(2,1)S(1)}, u32[]{:S(2)}, u32[]{:S(2)}) collective-permute-start(bf16[256,1152]{1,0:T(8,128)(2,1)S(1)} %collective-permute-done.3.p1), channel_id=1, source_target_pairs={{64,0},{128,64},{192,128},{32,192},{96,32},{160,96},{224,160},{416... | collective-permute-start | bytes 1769480 | tf_op jit(solution)/shard_map/ppermute | solution.py:58
  144.2 4.3 %collective-permute-done.6.c2 = bf16[256,1152]{1,0:T(8,128)(2,1)S(1)} collective-permute-done((bf16[256,1152]{1,0:T(8,128)(2,1)S(1)}, bf16[256,1152]{1,0:T(8,128)(2,1)S(1)}, u32[]{:S(2)}, u32[]{:S(2)}) %collective-permute-start.6) | collective-permute-done | bytes 589856 | tf_op jit(solution)/shard_map/ppermute | solution.py:58
  148.6 1.8 collective-permute-done.4.p2
  150.3 2.7 %gradients.1 = bf16[256,2304]{1,0:T(8,128)(2,1)S(1)} custom-call(f32[1]{0:T(128)S(6)} %copy.7.scale_ref, f32[1]{0:T(128)S(6)} %copy.8.offset_ref, bf16[256,1152]{1,0:T(8,128)(2,1)S(1)} %get-tuple-element.7.p0, bf16[256,1152]{1,0:T(8,128)(2,1)S(1)} %collective-permute-done.3.p1, bf16[256,1152]{1,0:T(8,128)(2,1)S(1)} %collective-permute-done.4.p2, ...), custom_call_target="tpu_custom_call" | custom-call | flops 1811939328 | bytes 4718592 | tf_op jit(solution)/shard_map/gradients/pallas_call | solution.py:96
  153.0 0.3 reshape.21
  153.3 31.9 %all_to_all.11 = bf16[64,4,2304]{2,1,0:T(4,128)(2,1)S(1)} all-to-all(bf16[64,4,2304]{2,1,0:T(4,128)(2,1)S(1)} %reshape.21), channel_id=1, replica_groups=mesh['grp'=16,'y_hi'=2,'z_hi'=16,'z_lo'=2] {'grp','y_hi','z_lo'}, dimensions={0} | all-to-all | bytes 2359296 | tf_op jit(solution)/shard_map/all_to_all | solution.py:122
  185.2 0.3 reshape.22
  185.5 0.4 convolution_convert_fusion.1
  185.9 7.9 %collective-permute-start.7 = (bf16[128,2304]{1,0:T(8,128)(2,1)S(1)}, bf16[128,2304]{1,0:T(8,128)(2,1)S(1)}, u32[]{:S(2)}, u32[]{:S(2)}) collective-permute-start(bf16[128,2304]{1,0:T(8,128)(2,1)S(1)} %convolution_convert_fusion.1), channel_id=1, source_target_pairs={{0,0},{129,1},{33,2},{161,3},{257,4},{385,5},{289,6},{417,7},{513,... | collective-permute-start | bytes 1769480 | tf_op jit(solution)/shard_map/ppermute | solution.py:58
  193.8 59.2 %collective-permute-done.7 = bf16[128,2304]{1,0:T(8,128)(2,1)S(1)} collective-permute-done((bf16[128,2304]{1,0:T(8,128)(2,1)S(1)}, bf16[128,2304]{1,0:T(8,128)(2,1)S(1)}, u32[]{:S(2)}, u32[]{:S(2)}) %collective-permute-start.7) | collective-permute-done | bytes 589856 | tf_op jit(solution)/shard_map/ppermute | solution.py:58
  253.1 0.9 fusion.5
  (1 shorter events, 0.0 us)
Async XLA Ops:
  0.6 3.4 %copy-start = (s32[128]{0:T(128)S(1)}, s32[128]{0:T(128)}, u32[]{:S(2)}) copy-start(s32[128]{0:T(128)} %param.7) | copy-start | bytes 1540
  1.7 30.9 %collective-permute-start = (bf16[128,2304]{1,0:T(8,128)(2,1)S(1)}, bf16[128,2304]{1,0:T(8,128)(2,1)S(1)}, u32[]{:S(2)}, u32[]{:S(2)}) collective-permute-start(bf16[128,2304]{1,0:T(8,128)(2,1)S(1)} %pad_maximum_fusion), channel_id=1, source_target_pairs={{0,0},{1,129},{2,34},{3,163},{4,260},{5,389},{6,294},{7,423},{8,52... | collective-permute-start | bytes 1769480 | tf_op jit(solution)/shard_map/ppermute | solution.py:58
  4.1 28.6 %collective-permute-start.1 = (s32[128]{0:T(128)S(1)}, s32[128]{0:T(128)S(1)}, u32[]{:S(2)}, u32[]{:S(2)}) collective-permute-start(s32[128]{0:T(128)S(1)} %copy-done), channel_id=1, source_target_pairs={{0,0},{1,129},{2,33},{3,161},{4,257},{5,385},{6,289},{7,417},{8,51... | collective-permute-start | bytes 1544 | tf_op jit(solution)/shard_map/ppermute | solution.py:58
  32.7 49.9 %collective-permute-start.2 = (bf16[128,2304]{1,0:T(8,128)(2,1)S(1)}, bf16[128,2304]{1,0:T(8,128)(2,1)S(1)}, u32[]{:S(2)}, u32[]{:S(2)}) collective-permute-start(bf16[128,2304]{1,0:T(8,128)(2,1)S(1)} %collective-permute-done), channel_id=1, source_target_pairs={{0,0},{129,129},{34,33},{163,161},{260,257},{389,385},{294,289},{4... | collective-permute-start | bytes 1769480 | tf_op jit(solution)/shard_map/ppermute | solution.py:58
  126.2 11.2 %collective-permute-start.5 = (bf16[256,1152]{1,0:T(8,128)(2,1)S(1)}, bf16[256,1152]{1,0:T(8,128)(2,1)S(1)}, u32[]{:S(2)}, u32[]{:S(2)}) collective-permute-start(bf16[256,1152]{1,0:T(8,128)(2,1)S(1)} %get-tuple-element.6.c0), channel_id=1, source_target_pairs={{0,64},{64,128},{128,192},{192,32},{32,96},{96,160},{160,224},{224... | collective-permute-start | bytes 1769480 | tf_op jit(solution)/shard_map/ppermute | solution.py:58
  128.4 10.9 %collective-permute-start.3 = (bf16[256,1152]{1,0:T(8,128)(2,1)S(1)}, bf16[256,1152]{1,0:T(8,128)(2,1)S(1)}, u32[]{:S(2)}, u32[]{:S(2)}) collective-permute-start(bf16[256,1152]{1,0:T(8,128)(2,1)S(1)} %get-tuple-element.7.p0), channel_id=1, source_target_pairs={{64,0},{128,64},{192,128},{32,192},{96,32},{160,96},{224,160},{416... | collective-permute-start | bytes 1769480 | tf_op jit(solution)/shard_map/ppermute | solution.py:58
  137.4 11.2 %collective-permute-start.6 = (bf16[256,1152]{1,0:T(8,128)(2,1)S(1)}, bf16[256,1152]{1,0:T(8,128)(2,1)S(1)}, u32[]{:S(2)}, u32[]{:S(2)}) collective-permute-start(bf16[256,1152]{1,0:T(8,128)(2,1)S(1)} %collective-permute-done.5.c1), channel_id=1, source_target_pairs={{0,64},{64,128},{128,192},{192,32},{32,96},{96,160},{160,224},{224... | collective-permute-start | bytes 1769480 | tf_op jit(solution)/shard_map/ppermute | solution.py:58
  139.3 11.0 %collective-permute-start.4 = (bf16[256,1152]{1,0:T(8,128)(2,1)S(1)}, bf16[256,1152]{1,0:T(8,128)(2,1)S(1)}, u32[]{:S(2)}, u32[]{:S(2)}) collective-permute-start(bf16[256,1152]{1,0:T(8,128)(2,1)S(1)} %collective-permute-done.3.p1), channel_id=1, source_target_pairs={{64,0},{128,64},{192,128},{32,192},{96,32},{160,96},{224,160},{416... | collective-permute-start | bytes 1769480 | tf_op jit(solution)/shard_map/ppermute | solution.py:58
  185.9 67.2 %collective-permute-start.7 = (bf16[128,2304]{1,0:T(8,128)(2,1)S(1)}, bf16[128,2304]{1,0:T(8,128)(2,1)S(1)}, u32[]{:S(2)}, u32[]{:S(2)}) collective-permute-start(bf16[128,2304]{1,0:T(8,128)(2,1)S(1)} %convolution_convert_fusion.1), channel_id=1, source_target_pairs={{0,0},{129,1},{33,2},{161,3},{257,4},{385,5},{289,6},{417,7},{513,... | collective-permute-start | bytes 1769480 | tf_op jit(solution)/shard_map/ppermute | solution.py:58

commit v7 on v5

--- a/solution.py
+++ b/solution.py
@@ -50,8 +50,10 @@
 
 
 OWNERS = [owner_device(owner) for owner in range(GRP * Y_HI * Z)]
-NEXT = [(OWNERS[i], OWNERS[(i + 1) % len(OWNERS)]) for i in range(len(OWNERS))]
-BEFORE = [(b, a) for a, b in NEXT]
+
+
+def owners_on(by):
+    return [(OWNERS[i], OWNERS[(i + by) % len(OWNERS)]) for i in range(len(OWNERS))]
 
 
 def moved(x, route):
@@ -61,7 +63,7 @@
 TILE = 384
 
 
-def gradients_kernel(scale_ref, offset_ref, p0, p1, p2, c0, c1, c2, out_ref):
+def gradients_kernel(scale_ref, offset_ref, p0, c0, p1, c1, p2, c2, out_ref):
     slots, width = p0.shape
     scale, offset = scale_ref[0], offset_ref[0]
     shape = (slots, slots)
@@ -91,7 +93,7 @@
 
 def gradients(scale, offset, pictures, captions):
     slots, width = pictures[0].shape
-    arrays = [*pictures, *captions]
+    arrays = [array for pair in zip(pictures, captions) for array in pair]
     flops = 12 * 2 * slots * slots * width
     return pl.pallas_call(
         gradients_kernel,
@@ -154,9 +156,9 @@
 
     earlier_captions = [captions]
     later_pictures = [pictures]
-    for _ in range(STEPS):
-        earlier_captions.append(moved(earlier_captions[-1], NEXT))
-        later_pictures.append(moved(later_pictures[-1], BEFORE))
+    for step in range(1, STEPS + 1):
+        later_pictures.append(moved(pictures, owners_on(-step)))
+        earlier_captions.append(moved(captions, owners_on(step)))
 
     done = gradients(score_scaling, score_offset_term, later_pictures, earlier_captions)
     back = swap_blocks(done, devices)

time: 254 us -> 256 us (level)
  the two profiles are of different devices: /device:TPU:20 before, /device:TPU:69 now
where the time goes in v7:
time: 256 us; the launch traced here: 255 us
  waiting for transfers between devices  116 us (45%)
  blocking collectives  67.1 us (26%)
  starting transfers between devices  62.7 us (24%)
  Pallas kernels  2.69 us (1%)
    ppermute x8, waiting for transfers between devices, moved(): return lax.ppermute(x, AXES, route)  116 us
    all_to_all x2, blocking collectives, swap_blocks(): lax.all_to_all(x.reshape(devices, slots // devices, width), REGION, split...  67.1 us
    ppermute x8, starting transfers between devices, moved(): return lax.ppermute(x, AXES, route)  62.7 us
  transfers between devices with their start and end apart: 8, of which 8 were waited for; matrix products, arithmetic and copies ran while one was open for 0% of the time, Pallas kernels for 0%

profile of v7, /device:TPU:69, one launch (start us, length us, event | category | flops | bytes accessed | tf_op | source)
XLA Modules:
  0.0 255.2 jit_solution(14675808904603313647)
XLA Ops:
  0.6 0.0 copy-start
  0.6 1.1 pad_maximum_fusion
  1.7 4.4 %collective-permute-start.1 = (bf16[128,2304]{1,0:T(8,128)(2,1)S(1)}, bf16[128,2304]{1,0:T(8,128)(2,1)S(1)}, u32[]{:S(2)}, u32[]{:S(2)}) collective-permute-start(bf16[128,2304]{1,0:T(8,128)(2,1)S(1)} %pad_maximum_fusion), channel_id=1, source_target_pairs={{0,0},{1,129},{2,34},{3,163},{4,260},{5,389},{6,294},{7,423},{8,52... | collective-permute-start | bytes 1769480 | tf_op jit(solution)/shard_map/ppermute | solution.py:60
  6.1 8.7 %collective-permute-done.1 = bf16[128,2304]{1,0:T(8,128)(2,1)S(1)} collective-permute-done((bf16[128,2304]{1,0:T(8,128)(2,1)S(1)}, bf16[128,2304]{1,0:T(8,128)(2,1)S(1)}, u32[]{:S(2)}, u32[]{:S(2)}) %collective-permute-start.1) | collective-permute-done | bytes 589856 | tf_op jit(solution)/shard_map/ppermute | solution.py:60
  14.8 24.8 %collective-permute-start.2 = (bf16[128,2304]{1,0:T(8,128)(2,1)S(1)}, bf16[128,2304]{1,0:T(8,128)(2,1)S(1)}, u32[]{:S(2)}, u32[]{:S(2)}) collective-permute-start(bf16[128,2304]{1,0:T(8,128)(2,1)S(1)} %collective-permute-done.1), channel_id=1, source_target_pairs={{0,0},{129,129},{34,33},{163,161},{260,257},{389,385},{294,289},{4... | collective-permute-start | bytes 1769480 | tf_op jit(solution)/shard_map/ppermute | solution.py:60
  39.6 0.0 copy-done
  39.6 13.3 %collective-permute-start = (s32[128]{0:T(128)S(1)}, s32[128]{0:T(128)S(1)}, u32[]{:S(2)}, u32[]{:S(2)}) collective-permute-start(s32[128]{0:T(128)S(1)} %copy-done), channel_id=1, source_target_pairs={{0,0},{1,129},{2,33},{3,161},{4,257},{5,385},{6,289},{7,417},{8,51... | collective-permute-start | bytes 1544 | tf_op jit(solution)/shard_map/ppermute | solution.py:60
  52.8 24.6 %collective-permute-done = s32[128]{0:T(128)S(1)} collective-permute-done((s32[128]{0:T(128)S(1)}, s32[128]{0:T(128)S(1)}, u32[]{:S(2)}, u32[]{:S(2)}) %collective-permute-start) | collective-permute-done | bytes 544 | tf_op jit(solution)/shard_map/ppermute | solution.py:60
  77.4 0.2 convert_reduce_fusion
  77.6 5.0 %collective-permute-done.2 = bf16[128,2304]{1,0:T(8,128)(2,1)S(1)} collective-permute-done((bf16[128,2304]{1,0:T(8,128)(2,1)S(1)}, bf16[128,2304]{1,0:T(8,128)(2,1)S(1)}, u32[]{:S(2)}, u32[]{:S(2)}) %collective-permute-start.2) | collective-permute-done | bytes 589856 | tf_op jit(solution)/shard_map/ppermute | solution.py:60
  82.7 0.5 convolution_convert_fusion
  83.1 0.3 reshape.19
  83.4 34.1 %all_to_all.10 = bf16[64,4,2304]{2,1,0:T(4,128)(2,1)S(1)} all-to-all(bf16[64,4,2304]{2,1,0:T(4,128)(2,1)S(1)} %reshape.19), channel_id=1, replica_groups=mesh['grp'=16,'y_hi'=2,'z_hi'=16,'z_lo'=2] {'grp','y_hi','z_lo'}, dimensions={0} | all-to-all | bytes 2359296 | tf_op jit(solution)/shard_map/all_to_all | solution.py:124
  117.6 0.3 reshape.20
  117.9 0.1 fusion.4
  118.0 2.5 collective-permute-start.6
  120.4 3.2 %collective-permute-start.4 = (bf16[256,1152]{1,0:T(8,128)(2,1)S(1)}, bf16[256,1152]{1,0:T(8,128)(2,1)S(1)}, u32[]{:S(2)}, u32[]{:S(2)}) collective-permute-start(bf16[256,1152]{1,0:T(8,128)(2,1)S(1)} %get-tuple-element.2.c0), channel_id=1, source_target_pairs={{0,64},{64,128},{128,192},{192,32},{32,96},{96,160},{160,224},{224... | collective-permute-start | bytes 1769480 | tf_op jit(solution)/shard_map/ppermute | solution.py:60
  123.7 3.6 %collective-permute-start.5 = (bf16[256,1152]{1,0:T(8,128)(2,1)S(1)}, bf16[256,1152]{1,0:T(8,128)(2,1)S(1)}, u32[]{:S(2)}, u32[]{:S(2)}) collective-permute-start(bf16[256,1152]{1,0:T(8,128)(2,1)S(1)} %get-tuple-element.3.p0), channel_id=1, source_target_pairs={{0,799},{64,863},{128,0},{192,64},{32,128},{96,192},{160,32},{224,... | collective-permute-start | bytes 1769480 | tf_op jit(solution)/shard_map/ppermute | solution.py:60
  127.3 2.0 collective-permute-start.3
  130.6 5.0 %collective-permute-done.6.c2 = bf16[256,1152]{1,0:T(8,128)(2,1)S(1)} collective-permute-done((bf16[256,1152]{1,0:T(8,128)(2,1)S(1)}, bf16[256,1152]{1,0:T(8,128)(2,1)S(1)}, u32[]{:S(2)}, u32[]{:S(2)}) %collective-permute-start.6) | collective-permute-done | bytes 589856 | tf_op jit(solution)/shard_map/ppermute | solution.py:60
  135.6 4.3 %collective-permute-done.4.c1 = bf16[256,1152]{1,0:T(8,128)(2,1)S(1)} collective-permute-done((bf16[256,1152]{1,0:T(8,128)(2,1)S(1)}, bf16[256,1152]{1,0:T(8,128)(2,1)S(1)}, u32[]{:S(2)}, u32[]{:S(2)}) %collective-permute-start.4) | collective-permute-done | bytes 589856 | tf_op jit(solution)/shard_map/ppermute | solution.py:60
  139.9 1.0 collective-permute-done.5.p2
  140.8 5.8 %collective-permute-done.3.p1 = bf16[256,1152]{1,0:T(8,128)(2,1)S(1)} collective-permute-done((bf16[256,1152]{1,0:T(8,128)(2,1)S(1)}, bf16[256,1152]{1,0:T(8,128)(2,1)S(1)}, u32[]{:S(2)}, u32[]{:S(2)}) %collective-permute-start.3) | collective-permute-done | bytes 589856 | tf_op jit(solution)/shard_map/ppermute | solution.py:60
  146.6 2.7 %gradients.1 = bf16[256,2304]{1,0:T(8,128)(2,1)S(1)} custom-call(f32[1]{0:T(128)S(6)} %copy.7.scale_ref, f32[1]{0:T(128)S(6)} %copy.8.offset_ref, bf16[256,1152]{1,0:T(8,128)(2,1)S(1)} %get-tuple-element.3.p0, bf16[256,1152]{1,0:T(8,128)(2,1)S(1)} %get-tuple-element.2.c0, bf16[256,1152]{1,0:T(8,128)(2,1)S(1)} %collective-permute-done.3.p1, ...), custom_call_target="tpu_custom_call" | custom-call | flops 1811939328 | bytes 4718592 | tf_op jit(solution)/shard_map/gradients/pallas_call | solution.py:98
  149.3 0.3 reshape.21
  149.6 33.0 %all_to_all.11 = bf16[64,4,2304]{2,1,0:T(4,128)(2,1)S(1)} all-to-all(bf16[64,4,2304]{2,1,0:T(4,128)(2,1)S(1)} %reshape.21), channel_id=1, replica_groups=mesh['grp'=16,'y_hi'=2,'z_hi'=16,'z_lo'=2] {'grp','y_hi','z_lo'}, dimensions={0} | all-to-all | bytes 2359296 | tf_op jit(solution)/shard_map/all_to_all | solution.py:124
  182.6 0.3 reshape.22
  182.9 0.4 convolution_convert_fusion.1
  183.3 9.0 %collective-permute-start.7 = (bf16[128,2304]{1,0:T(8,128)(2,1)S(1)}, bf16[128,2304]{1,0:T(8,128)(2,1)S(1)}, u32[]{:S(2)}, u32[]{:S(2)}) collective-permute-start(bf16[128,2304]{1,0:T(8,128)(2,1)S(1)} %convolution_convert_fusion.1), channel_id=1, source_target_pairs={{0,0},{129,1},{33,2},{161,3},{257,4},{385,5},{289,6},{417,7},{513,... | collective-permute-start | bytes 1769480 | tf_op jit(solution)/shard_map/ppermute | solution.py:60
  192.3 62.0 %collective-permute-done.7 = bf16[128,2304]{1,0:T(8,128)(2,1)S(1)} collective-permute-done((bf16[128,2304]{1,0:T(8,128)(2,1)S(1)}, bf16[128,2304]{1,0:T(8,128)(2,1)S(1)}, u32[]{:S(2)}, u32[]{:S(2)}) %collective-permute-start.7) | collective-permute-done | bytes 589856 | tf_op jit(solution)/shard_map/ppermute | solution.py:60
  254.4 0.9 fusion.5
  (1 shorter events, 0.0 us)
Async XLA Ops:
  0.6 38.9 %copy-start = (s32[128]{0:T(128)S(1)}, s32[128]{0:T(128)}, u32[]{:S(2)}) copy-start(s32[128]{0:T(128)} %param.7) | copy-start | bytes 1540
  1.7 13.1 %collective-permute-start.1 = (bf16[128,2304]{1,0:T(8,128)(2,1)S(1)}, bf16[128,2304]{1,0:T(8,128)(2,1)S(1)}, u32[]{:S(2)}, u32[]{:S(2)}) collective-permute-start(bf16[128,2304]{1,0:T(8,128)(2,1)S(1)} %pad_maximum_fusion), channel_id=1, source_target_pairs={{0,0},{1,129},{2,34},{3,163},{4,260},{5,389},{6,294},{7,423},{8,52... | collective-permute-start | bytes 1769480 | tf_op jit(solution)/shard_map/ppermute | solution.py:60
  14.8 67.9 %collective-permute-start.2 = (bf16[128,2304]{1,0:T(8,128)(2,1)S(1)}, bf16[128,2304]{1,0:T(8,128)(2,1)S(1)}, u32[]{:S(2)}, u32[]{:S(2)}) collective-permute-start(bf16[128,2304]{1,0:T(8,128)(2,1)S(1)} %collective-permute-done.1), channel_id=1, source_target_pairs={{0,0},{129,129},{34,33},{163,161},{260,257},{389,385},{294,289},{4... | collective-permute-start | bytes 1769480 | tf_op jit(solution)/shard_map/ppermute | solution.py:60
  39.6 37.8 %collective-permute-start = (s32[128]{0:T(128)S(1)}, s32[128]{0:T(128)S(1)}, u32[]{:S(2)}, u32[]{:S(2)}) collective-permute-start(s32[128]{0:T(128)S(1)} %copy-done), channel_id=1, source_target_pairs={{0,0},{1,129},{2,33},{3,161},{4,257},{5,385},{6,289},{7,417},{8,51... | collective-permute-start | bytes 1544 | tf_op jit(solution)/shard_map/ppermute | solution.py:60
  118.0 17.6 %collective-permute-start.6 = (bf16[256,1152]{1,0:T(8,128)(2,1)S(1)}, bf16[256,1152]{1,0:T(8,128)(2,1)S(1)}, u32[]{:S(2)}, u32[]{:S(2)}) collective-permute-start(bf16[256,1152]{1,0:T(8,128)(2,1)S(1)} %get-tuple-element.2.c0), channel_id=1, source_target_pairs={{0,128},{64,192},{128,32},{192,96},{32,160},{96,224},{160,416},{22... | collective-permute-start | bytes 1769480 | tf_op jit(solution)/shard_map/ppermute | solution.py:60
  120.4 19.4 %collective-permute-start.4 = (bf16[256,1152]{1,0:T(8,128)(2,1)S(1)}, bf16[256,1152]{1,0:T(8,128)(2,1)S(1)}, u32[]{:S(2)}, u32[]{:S(2)}) collective-permute-start(bf16[256,1152]{1,0:T(8,128)(2,1)S(1)} %get-tuple-element.2.c0), channel_id=1, source_target_pairs={{0,64},{64,128},{128,192},{192,32},{32,96},{96,160},{160,224},{224... | collective-permute-start | bytes 1769480 | tf_op jit(solution)/shard_map/ppermute | solution.py:60
  123.7 17.1 %collective-permute-start.5 = (bf16[256,1152]{1,0:T(8,128)(2,1)S(1)}, bf16[256,1152]{1,0:T(8,128)(2,1)S(1)}, u32[]{:S(2)}, u32[]{:S(2)}) collective-permute-start(bf16[256,1152]{1,0:T(8,128)(2,1)S(1)} %get-tuple-element.3.p0), channel_id=1, source_target_pairs={{0,799},{64,863},{128,0},{192,64},{32,128},{96,192},{160,32},{224,... | collective-permute-start | bytes 1769480 | tf_op jit(solution)/shard_map/ppermute | solution.py:60
  127.3 19.3 %collective-permute-start.3 = (bf16[256,1152]{1,0:T(8,128)(2,1)S(1)}, bf16[256,1152]{1,0:T(8,128)(2,1)S(1)}, u32[]{:S(2)}, u32[]{:S(2)}) collective-permute-start(bf16[256,1152]{1,0:T(8,128)(2,1)S(1)} %get-tuple-element.3.p0), channel_id=1, source_target_pairs={{0,863},{64,0},{128,64},{192,128},{32,192},{96,32},{160,96},{224,1... | collective-permute-start | bytes 1769480 | tf_op jit(solution)/shard_map/ppermute | solution.py:60
  183.3 71.1 %collective-permute-start.7 = (bf16[128,2304]{1,0:T(8,128)(2,1)S(1)}, bf16[128,2304]{1,0:T(8,128)(2,1)S(1)}, u32[]{:S(2)}, u32[]{:S(2)}) collective-permute-start(bf16[128,2304]{1,0:T(8,128)(2,1)S(1)} %convolution_convert_fusion.1), channel_id=1, source_target_pairs={{0,0},{129,1},{33,2},{161,3},{257,4},{385,5},{289,6},{417,7},{513,... | collective-permute-start | bytes 1769480 | tf_op jit(solution)/shard_map/ppermute | solution.py:60

commit v8 on v5

--- a/solution.py
+++ b/solution.py
@@ -160,8 +160,10 @@
 
     done = gradients(score_scaling, score_offset_term, later_pictures, earlier_captions)
     back = swap_blocks(done, devices)
-    grads = moved(rows_of_transpose(placer, back).astype(jnp.bfloat16), FROM_REGION)
-    return (grads[:, :width], grads[:, width:])
+    grads = rows_of_transpose(placer, back).astype(jnp.bfloat16)
+    image_grad = moved(grads[:, :width], FROM_REGION)
+    text_grad = moved(grads[:, width:], FROM_REGION)
+    return (image_grad, text_grad)
 
 
 def solution(mesh):

time: 254 us -> 254 us (level)
  the two profiles are of different devices: /device:TPU:20 before, /device:TPU:76 now
where the time goes in v8:
time: 254 us
  waiting for transfers between devices  105 us (41%)
  starting transfers between devices  71.2 us (28%)
  blocking collectives  67.7 us (27%)
  local copies, waits for them, and re-layouts  2.78 us (1%)
  Pallas kernels  2.69 us (1%)
    ppermute x9, waiting for transfers between devices, moved(): return lax.ppermute(x, AXES, route)  105 us
    ppermute x9, starting transfers between devices, moved(): return lax.ppermute(x, AXES, route)  71.2 us
    all_to_all x2, blocking collectives, swap_blocks(): lax.all_to_all(x.reshape(devices, slots // devices, width), REGION, split...  67.7 us
  transfers between devices with their start and end apart: 9, of which 8 were waited for; matrix products, arithmetic and copies ran while one was open for 0% of the time, Pallas kernels for 0%

profile of v8, /device:TPU:76, one launch (start us, length us, event | category | flops | bytes accessed | tf_op | source)
XLA Modules:
  0.0 253.8 jit_solution(16241890488989814656)
XLA Ops:
  0.6 0.0 copy-start
  0.6 1.1 pad_maximum_fusion
  1.7 2.3 collective-permute-start.1
  4.1 13.3 %collective-permute-done.1 = bf16[128,2304]{1,0:T(8,128)(2,1)S(1)} collective-permute-done((bf16[128,2304]{1,0:T(8,128)(2,1)S(1)}, bf16[128,2304]{1,0:T(8,128)(2,1)S(1)}, u32[]{:S(2)}, u32[]{:S(2)}) %collective-permute-start.1) | collective-permute-done | bytes 589856 | tf_op jit(solution)/shard_map/ppermute | solution.py:58
  17.3 5.9 %collective-permute-start.2 = (bf16[128,2304]{1,0:T(8,128)(2,1)S(1)}, bf16[128,2304]{1,0:T(8,128)(2,1)S(1)}, u32[]{:S(2)}, u32[]{:S(2)}) collective-permute-start(bf16[128,2304]{1,0:T(8,128)(2,1)S(1)} %collective-permute-done.1), channel_id=1, source_target_pairs={{0,0},{129,129},{34,33},{163,161},{260,257},{389,385},{294,289},{4... | collective-permute-start | bytes 1769480 | tf_op jit(solution)/shard_map/ppermute | solution.py:58
  23.2 0.0 copy-done
  23.2 27.2 %collective-permute-start = (s32[128]{0:T(128)S(1)}, s32[128]{0:T(128)S(1)}, u32[]{:S(2)}, u32[]{:S(2)}) collective-permute-start(s32[128]{0:T(128)S(1)} %copy-done), channel_id=1, source_target_pairs={{0,0},{1,129},{2,33},{3,161},{4,257},{5,385},{6,289},{7,417},{8,51... | collective-permute-start | bytes 1544 | tf_op jit(solution)/shard_map/ppermute | solution.py:58
  50.4 5.9 %collective-permute-done = s32[128]{0:T(128)S(1)} collective-permute-done((s32[128]{0:T(128)S(1)}, s32[128]{0:T(128)S(1)}, u32[]{:S(2)}, u32[]{:S(2)}) %collective-permute-start) | collective-permute-done | bytes 544 | tf_op jit(solution)/shard_map/ppermute | solution.py:58
  56.3 0.2 convert_reduce_fusion
  56.5 29.0 %collective-permute-done.2 = bf16[128,2304]{1,0:T(8,128)(2,1)S(1)} collective-permute-done((bf16[128,2304]{1,0:T(8,128)(2,1)S(1)}, bf16[128,2304]{1,0:T(8,128)(2,1)S(1)}, u32[]{:S(2)}, u32[]{:S(2)}) %collective-permute-start.2) | collective-permute-done | bytes 589856 | tf_op jit(solution)/shard_map/ppermute | solution.py:58
  85.5 0.5 convolution_convert_fusion
  86.0 0.3 reshape.19
  86.3 30.0 %all_to_all.10 = bf16[64,4,2304]{2,1,0:T(4,128)(2,1)S(1)} all-to-all(bf16[64,4,2304]{2,1,0:T(4,128)(2,1)S(1)} %reshape.19), channel_id=1, replica_groups=mesh['grp'=16,'y_hi'=2,'z_hi'=16,'z_lo'=2] {'grp','y_hi','z_lo'}, dimensions={0} | all-to-all | bytes 2359296 | tf_op jit(solution)/shard_map/all_to_all | solution.py:122
  116.3 0.3 reshape.20
  116.6 0.1 fusion.4
  116.7 2.3 collective-permute-start.5
  119.0 3.3 %collective-permute-start.3 = (bf16[256,1152]{1,0:T(8,128)(2,1)S(1)}, bf16[256,1152]{1,0:T(8,128)(2,1)S(1)}, u32[]{:S(2)}, u32[]{:S(2)}) collective-permute-start(bf16[256,1152]{1,0:T(8,128)(2,1)S(1)} %get-tuple-element.3.p0), channel_id=1, source_target_pairs={{64,0},{128,64},{192,128},{32,192},{96,32},{160,96},{224,160},{416... | collective-permute-start | bytes 1769480 | tf_op jit(solution)/shard_map/ppermute | solution.py:58
  122.3 5.6 %collective-permute-done.5.c1 = bf16[256,1152]{1,0:T(8,128)(2,1)S(1)} collective-permute-done((bf16[256,1152]{1,0:T(8,128)(2,1)S(1)}, bf16[256,1152]{1,0:T(8,128)(2,1)S(1)}, u32[]{:S(2)}, u32[]{:S(2)}) %collective-permute-start.5) | collective-permute-done | bytes 589856 | tf_op jit(solution)/shard_map/ppermute | solution.py:58
  127.9 1.9 collective-permute-start.6
  129.8 0.0 collective-permute-done.3.p1
  129.8 3.6 %collective-permute-start.4 = (bf16[256,1152]{1,0:T(8,128)(2,1)S(1)}, bf16[256,1152]{1,0:T(8,128)(2,1)S(1)}, u32[]{:S(2)}, u32[]{:S(2)}) collective-permute-start(bf16[256,1152]{1,0:T(8,128)(2,1)S(1)} %collective-permute-done.3.p1), channel_id=1, source_target_pairs={{64,0},{128,64},{192,128},{32,192},{96,32},{160,96},{224,160},{416... | collective-permute-start | bytes 1769480 | tf_op jit(solution)/shard_map/ppermute | solution.py:58
  134.8 4.3 %collective-permute-done.6.c2 = bf16[256,1152]{1,0:T(8,128)(2,1)S(1)} collective-permute-done((bf16[256,1152]{1,0:T(8,128)(2,1)S(1)}, bf16[256,1152]{1,0:T(8,128)(2,1)S(1)}, u32[]{:S(2)}, u32[]{:S(2)}) %collective-permute-start.6) | collective-permute-done | bytes 589856 | tf_op jit(solution)/shard_map/ppermute | solution.py:58
  139.1 1.8 collective-permute-done.4.p2
  140.9 2.7 %gradients.1 = bf16[256,2304]{1,0:T(8,128)(2,1)S(1)} custom-call(f32[1]{0:T(128)S(6)} %copy.9.scale_ref, f32[1]{0:T(128)S(6)} %copy.10.offset_ref, bf16[256,1152]{1,0:T(8,128)(2,1)S(1)} %get-tuple-element.3.p0, bf16[256,1152]{1,0:T(8,128)(2,1)S(1)} %collective-permute-done.3.p1, bf16[256,1152]{1,0:T(8,128)(2,1)S(1)} %collective-permute-done.4.p2, ...), custom_call_target="tpu_custom_call" | custom-call | flops 1811939328 | bytes 4718592 | tf_op jit(solution)/shard_map/gradients/pallas_call | solution.py:96
  143.6 0.3 reshape.21
  143.9 37.7 %all_to_all.11 = bf16[64,4,2304]{2,1,0:T(4,128)(2,1)S(1)} all-to-all(bf16[64,4,2304]{2,1,0:T(4,128)(2,1)S(1)} %reshape.21), channel_id=1, replica_groups=mesh['grp'=16,'y_hi'=2,'z_hi'=16,'z_lo'=2] {'grp','y_hi','z_lo'}, dimensions={0} | all-to-all | bytes 2359296 | tf_op jit(solution)/shard_map/all_to_all | solution.py:122
  181.5 0.3 reshape.22
  181.8 0.4 convolution_convert_fusion.1
  182.3 10.5 %collective-permute-start.8 = (bf16[128,1152]{1,0:T(8,128)(2,1)S(1)}, bf16[128,1152]{1,0:T(8,128)(2,1)S(1)}, u32[]{:S(2)}, u32[]{:S(2)}) collective-permute-start(bf16[128,1152]{1,0:T(8,128)(2,1)S(1)} %get-tuple-element.4), channel_id=1, source_target_pairs={{0,0},{129,1},{33,2},{161,3},{257,4},{385,5},{289,6},{417,7},{513,... | collective-permute-start | bytes 884744 | tf_op jit(solution)/shard_map/ppermute | solution.py:58
  192.7 14.2 %collective-permute-start.7 = (bf16[128,1152]{1,0:T(8,128)(2,1)S(1)}, bf16[128,1152]{1,0:T(8,128)(2,1)S(1)}, u32[]{:S(2)}, u32[]{:S(2)}) collective-permute-start(bf16[128,1152]{1,0:T(8,128)(2,1)S(1)} %get-tuple-element.5), channel_id=1, source_target_pairs={{0,0},{129,1},{33,2},{161,3},{257,4},{385,5},{289,6},{417,7},{513,... | collective-permute-start | bytes 884744 | tf_op jit(solution)/shard_map/ppermute | solution.py:58
  207.0 25.5 %collective-permute-done.8 = bf16[128,1152]{1,0:T(8,128)(2,1)S(1)} collective-permute-done((bf16[128,1152]{1,0:T(8,128)(2,1)S(1)}, bf16[128,1152]{1,0:T(8,128)(2,1)S(1)}, u32[]{:S(2)}, u32[]{:S(2)}) %collective-permute-start.8) | collective-permute-done | bytes 294944 | tf_op jit(solution)/shard_map/ppermute | solution.py:58
  232.5 19.9 %collective-permute-done.7 = bf16[128,1152]{1,0:T(8,128)(2,1)S(1)} collective-permute-done((bf16[128,1152]{1,0:T(8,128)(2,1)S(1)}, bf16[128,1152]{1,0:T(8,128)(2,1)S(1)}, u32[]{:S(2)}, u32[]{:S(2)}) %collective-permute-start.7) | collective-permute-done | bytes 294944 | tf_op jit(solution)/shard_map/ppermute | solution.py:58
  252.4 0.7 copy.11
  253.1 0.7 copy.12
  (2 shorter events, 0.1 us)
Async XLA Ops:
  0.6 22.6 %copy-start = (s32[128]{0:T(128)S(1)}, s32[128]{0:T(128)}, u32[]{:S(2)}) copy-start(s32[128]{0:T(128)} %param.7) | copy-start | bytes 1540
  1.7 15.6 %collective-permute-start.1 = (bf16[128,2304]{1,0:T(8,128)(2,1)S(1)}, bf16[128,2304]{1,0:T(8,128)(2,1)S(1)}, u32[]{:S(2)}, u32[]{:S(2)}) collective-permute-start(bf16[128,2304]{1,0:T(8,128)(2,1)S(1)} %pad_maximum_fusion), channel_id=1, source_target_pairs={{0,0},{1,129},{2,34},{3,163},{4,260},{5,389},{6,294},{7,423},{8,52... | collective-permute-start | bytes 1769480 | tf_op jit(solution)/shard_map/ppermute | solution.py:58
  17.3 68.2 %collective-permute-start.2 = (bf16[128,2304]{1,0:T(8,128)(2,1)S(1)}, bf16[128,2304]{1,0:T(8,128)(2,1)S(1)}, u32[]{:S(2)}, u32[]{:S(2)}) collective-permute-start(bf16[128,2304]{1,0:T(8,128)(2,1)S(1)} %collective-permute-done.1), channel_id=1, source_target_pairs={{0,0},{129,129},{34,33},{163,161},{260,257},{389,385},{294,289},{4... | collective-permute-start | bytes 1769480 | tf_op jit(solution)/shard_map/ppermute | solution.py:58
  23.2 33.0 %collective-permute-start = (s32[128]{0:T(128)S(1)}, s32[128]{0:T(128)S(1)}, u32[]{:S(2)}, u32[]{:S(2)}) collective-permute-start(s32[128]{0:T(128)S(1)} %copy-done), channel_id=1, source_target_pairs={{0,0},{1,129},{2,33},{3,161},{4,257},{5,385},{6,289},{7,417},{8,51... | collective-permute-start | bytes 1544 | tf_op jit(solution)/shard_map/ppermute | solution.py:58
  116.7 11.2 %collective-permute-start.5 = (bf16[256,1152]{1,0:T(8,128)(2,1)S(1)}, bf16[256,1152]{1,0:T(8,128)(2,1)S(1)}, u32[]{:S(2)}, u32[]{:S(2)}) collective-permute-start(bf16[256,1152]{1,0:T(8,128)(2,1)S(1)} %get-tuple-element.2.c0), channel_id=1, source_target_pairs={{0,64},{64,128},{128,192},{192,32},{32,96},{96,160},{160,224},{224... | collective-permute-start | bytes 1769480 | tf_op jit(solution)/shard_map/ppermute | solution.py:58
  119.0 10.9 %collective-permute-start.3 = (bf16[256,1152]{1,0:T(8,128)(2,1)S(1)}, bf16[256,1152]{1,0:T(8,128)(2,1)S(1)}, u32[]{:S(2)}, u32[]{:S(2)}) collective-permute-start(bf16[256,1152]{1,0:T(8,128)(2,1)S(1)} %get-tuple-element.3.p0), channel_id=1, source_target_pairs={{64,0},{128,64},{192,128},{32,192},{96,32},{160,96},{224,160},{416... | collective-permute-start | bytes 1769480 | tf_op jit(solution)/shard_map/ppermute | solution.py:58
  127.9 11.2 %collective-permute-start.6 = (bf16[256,1152]{1,0:T(8,128)(2,1)S(1)}, bf16[256,1152]{1,0:T(8,128)(2,1)S(1)}, u32[]{:S(2)}, u32[]{:S(2)}) collective-permute-start(bf16[256,1152]{1,0:T(8,128)(2,1)S(1)} %collective-permute-done.5.c1), channel_id=1, source_target_pairs={{0,64},{64,128},{128,192},{192,32},{32,96},{96,160},{160,224},{224... | collective-permute-start | bytes 1769480 | tf_op jit(solution)/shard_map/ppermute | solution.py:58
  129.8 11.0 %collective-permute-start.4 = (bf16[256,1152]{1,0:T(8,128)(2,1)S(1)}, bf16[256,1152]{1,0:T(8,128)(2,1)S(1)}, u32[]{:S(2)}, u32[]{:S(2)}) collective-permute-start(bf16[256,1152]{1,0:T(8,128)(2,1)S(1)} %collective-permute-done.3.p1), channel_id=1, source_target_pairs={{64,0},{128,64},{192,128},{32,192},{96,32},{160,96},{224,160},{416... | collective-permute-start | bytes 1769480 | tf_op jit(solution)/shard_map/ppermute | solution.py:58
  182.3 50.2 %collective-permute-start.8 = (bf16[128,1152]{1,0:T(8,128)(2,1)S(1)}, bf16[128,1152]{1,0:T(8,128)(2,1)S(1)}, u32[]{:S(2)}, u32[]{:S(2)}) collective-permute-start(bf16[128,1152]{1,0:T(8,128)(2,1)S(1)} %get-tuple-element.4), channel_id=1, source_target_pairs={{0,0},{129,1},{33,2},{161,3},{257,4},{385,5},{289,6},{417,7},{513,... | collective-permute-start | bytes 884744 | tf_op jit(solution)/shard_map/ppermute | solution.py:58
  192.7 59.7 %collective-permute-start.7 = (bf16[128,1152]{1,0:T(8,128)(2,1)S(1)}, bf16[128,1152]{1,0:T(8,128)(2,1)S(1)}, u32[]{:S(2)}, u32[]{:S(2)}) collective-permute-start(bf16[128,1152]{1,0:T(8,128)(2,1)S(1)} %get-tuple-element.5), channel_id=1, source_target_pairs={{0,0},{129,1},{33,2},{161,3},{257,4},{385,5},{289,6},{417,7},{513,... | collective-permute-start | bytes 884744 | tf_op jit(solution)/shard_map/ppermute | solution.py:58
